TPU v7x, 256 devices: a whole 4x4x8 slice. The times are simulated.
256 devices in a mesh: dp: 4 (over y_hi, core), expert: 64 (over x, z, y_lo).
Axes of the slice: x: 4, y: 4 (y_hi: 2, y_lo: 2; y = y_hi * 2 + y_lo), z: 8, core: 2. Of those that a mesh axis runs over, the one named last changes fastest.
Arguments:
- tokens: bfloat16 [32768, 2048], P(('dp', 'expert')), may hold values from -6 to 6
- cotangent: bfloat16 [32768, 2048], P(('dp', 'expert')), may hold values from -6 to 6
- routes: int32 [32768, 3], P(('dp', 'expert')), may hold values from 0 to 63, as said below
- slot_index: int32 [32768, 3], P(('dp', 'expert')), may hold values from 0 to 7, as said below
- route_weight: float32 [32768, 3], P(('dp', 'expert')), may hold values from 0.05 to 0.6
- swap_flags: int32 [64], replicated, may hold values from 0 to 1, as said below
- w_gate_up: bfloat16 [64, 2048, 1536], P('expert', 'dp'), may hold values from -0.125 to 0.125
- w_down: bfloat16 [64, 768, 2048], P('expert', 'dp'), may hold values from -0.21875 to 0.21875
Outputs:
- grad_tokens: float32 [32768, 2048], P(('dp', 'expert'))
- grad_weight: float32 [32768, 3], P(('dp', 'expert'))
- grad_gate_up: float32 [64, 2048, 1536], P('expert', 'dp')
- grad_down: float32 [64, 768, 2048], P('expert', 'dp')
Inputs may be any that keep to these rules, and one draw needn't show every extreme that they name: `routes`: each token names 3 different experts. Within each aligned block of 128 tokens (the tokens of one device) no expert is named more than 8 times, and one expert, the same in every block, is named exactly 8 times in every block. `slot_index`: within each aligned block of 128 tokens, the assignments to one expert have distinct slots. swap_flags[e] equals swap_flags[e XOR (32)], and swap_flags[63] is 1.
All inputs are finite; a program needn't handle non-finite values.
Results may differ from a plain program's by a relative error of at most 0.011.
Values may be sent and summed in bfloat16 or wider, within the bound.
A program may use at most 128 MiB of HBM per device.

v0:
```python
import jax
import jax.numpy as jnp
from jax import lax
from jax.sharding import PartitionSpec as P


def swapped(shard, axis, distance):
    return lax.ppermute(shard, axis, [(i, i ^ 1 << distance) for i in range(lax.axis_size(axis))])


def forward_pass(rows_in, gate_up_w, down_w):
    width = down_w.shape[0]
    gate_up = jnp.dot(rows_in, gate_up_w, preferred_element_type=jnp.float32)
    gate = gate_up[:, :width]
    up_val = gate_up[:, width:]
    sigmoid_gate = jax.nn.sigmoid(gate)
    silu_gate = gate * sigmoid_gate
    hidden_act = (silu_gate * up_val).astype(jnp.bfloat16)
    expert_out = jnp.dot(hidden_act, down_w, preferred_element_type=jnp.float32)
    return (gate, up_val, sigmoid_gate, silu_gate, hidden_act, expert_out)


def backward_pass(forward_vals, cot_in, weight_in, gate_up_w, down_w):
    gate, up_val, sigmoid_gate, silu_gate, hidden_act, expert_out = forward_vals
    prob_grad = jnp.sum(expert_out * cot_in.astype(jnp.float32), axis=1).astype(jnp.bfloat16)
    scaled = (weight_in.astype(jnp.float32)[:, None] * cot_in.astype(jnp.float32)).astype(
        jnp.bfloat16
    )
    hidden_grad = lax.dot_general(
        scaled, down_w, (((1,), (1,)), ((), ())), preferred_element_type=jnp.float32
    )
    gate_grad = (hidden_grad * up_val * sigmoid_gate * (1.0 + gate * (1.0 - sigmoid_gate))).astype(
        jnp.bfloat16
    )
    up_grad = (hidden_grad * silu_gate).astype(jnp.bfloat16)
    both_grad = jnp.concatenate([gate_grad, up_grad], axis=1)
    row_grad = lax.dot_general(
        both_grad, gate_up_w, (((1,), (1,)), ((), ())), preferred_element_type=jnp.float32
    ).astype(jnp.bfloat16)
    return (hidden_act, scaled, both_grad, row_grad, prob_grad)


def body(tokens, cotangent, routes, slot_index, route_weight, swap_flags, w_gate_up, w_down):
    count_dev = lax.axis_size("expert")
    half_axis = count_dev // 2
    swap_bit = half_axis.bit_length() - 1
    tok_rows, model_width = tokens.shape
    top_count = routes.shape[1]
    capacity = tok_rows * top_count * 4 // (3 * count_dev)
    buffer_rows = count_dev * capacity
    expert_ids = jnp.arange(count_dev, dtype=jnp.int32)
    my_index = lax.axis_index("expert")
    my_flag = jnp.sum(jnp.where(expert_ids == my_index, swap_flags, 0))
    row_index = (routes * capacity + slot_index).reshape(-1)
    assign_count = tok_rows * top_count
    assign_ids = jnp.arange(assign_count, dtype=jnp.int32)
    source_row = (
        jnp.full((buffer_rows,), tok_rows, jnp.int32).at[row_index].set(assign_ids // top_count)
    )
    assign_of_row = jnp.full((buffer_rows,), assign_count, jnp.int32).at[row_index].set(assign_ids)
    padded_tokens = jnp.concatenate([tokens, jnp.zeros((1, model_width), jnp.bfloat16)], axis=0)
    padded_cot = jnp.concatenate([cotangent, jnp.zeros((1, model_width), jnp.bfloat16)], axis=0)
    weight_flat = jnp.concatenate(
        [route_weight.astype(jnp.bfloat16).reshape(-1), jnp.zeros((1,), jnp.bfloat16)]
    )
    send_rows = padded_tokens[source_row].reshape(count_dev, capacity, model_width)
    send_cot = padded_cot[source_row].reshape(count_dev, capacity, model_width)
    send_weight = weight_flat[assign_of_row].reshape(count_dev, capacity)
    gate_up_full, down_full = (
        lax.all_gather(w_gate_up, "dp", axis=1, tiled=True),
        lax.all_gather(w_down, "dp", axis=1, tiled=True),
    )
    gate_up_full = gate_up_full[0]
    down_full = down_full[0]
    recv_rows, recv_cot, recv_weight = (
        lax.all_to_all(send_rows, "expert", split_axis=0, concat_axis=0, tiled=True),
        lax.all_to_all(send_cot, "expert", split_axis=0, concat_axis=0, tiled=True),
        lax.all_to_all(send_weight, "expert", split_axis=0, concat_axis=0, tiled=True),
    )
    rows_in = recv_rows.reshape(buffer_rows, model_width)
    forward_vals = forward_pass(rows_in, gate_up_full, down_full)
    cot_in = recv_cot.reshape(buffer_rows, model_width)
    weight_in = recv_weight.reshape(buffer_rows)
    hidden_act, scaled, both_grad, row_grad, prob_grad = backward_pass(
        forward_vals, cot_in, weight_in, gate_up_full, down_full
    )
    back_rows, back_prob = (
        lax.all_to_all(
            row_grad.reshape(count_dev, capacity, model_width),
            "expert",
            split_axis=0,
            concat_axis=0,
            tiled=True,
        ),
        lax.all_to_all(
            prob_grad.reshape(count_dev, capacity),
            "expert",
            split_axis=0,
            concat_axis=0,
            tiled=True,
        ),
    )
    picked_rows = back_rows.reshape(buffer_rows, model_width)[row_index]
    grad_tokens = jnp.sum(
        picked_rows.astype(jnp.float32).reshape(tok_rows, top_count, model_width), axis=1
    )
    grad_weight = (
        back_prob.reshape(buffer_rows)[row_index].astype(jnp.float32).reshape(tok_rows, top_count)
    )
    part = rows_in
    term = lax.dot_general(
        part, both_grad, (((0,), (0,)), ((), ())), preferred_element_type=jnp.float32
    )
    grad_gu = lax.psum_scatter(
        lax.optimization_barrier(term.astype(jnp.bfloat16))
        .astype(jnp.float32)
        .astype(jnp.bfloat16),
        "dp",
        scatter_dimension=0,
        tiled=True,
    ).astype(jnp.float32)[None]
    part = hidden_act
    term = lax.dot_general(
        part, scaled, (((0,), (0,)), ((), ())), preferred_element_type=jnp.float32
    )
    grad_dn = lax.psum_scatter(
        lax.optimization_barrier(term.astype(jnp.bfloat16))
        .astype(jnp.float32)
        .astype(jnp.bfloat16),
        "dp",
        scatter_dimension=0,
        tiled=True,
    ).astype(jnp.float32)[None]
    partner_grads = (
        swapped(grad_gu.astype(jnp.bfloat16), "expert", swap_bit).astype(grad_gu.dtype),
        swapped(grad_dn.astype(jnp.bfloat16), "expert", swap_bit).astype(grad_dn.dtype),
    )
    grad_gu = jnp.where(my_flag == 1, partner_grads[0], grad_gu)
    grad_dn = jnp.where(my_flag == 1, partner_grads[1], grad_dn)
    return (grad_tokens, grad_weight, grad_gu, grad_dn)


def solution(mesh):
    return jax.shard_map(
        body,
        mesh=mesh,
        in_specs=(
            P(("dp", "expert"), None),
            P(("dp", "expert"), None),
            P(("dp", "expert"), None),
            P(("dp", "expert"), None),
            P(("dp", "expert"), None),
            P(),
            P("expert", "dp", None),
            P("expert", "dp", None),
        ),
        out_specs=(
            P(("dp", "expert"), None),
            P(("dp", "expert"), None),
            P("expert", "dp", None),
            P("expert", "dp", None),
        ),
        check_vma=False,
    )
```

profile of v0, /device:TPU:1, one launch (start us, length us, event | category | flops | bytes accessed | tf_op | source)
XLA Modules:
  0.0 345.9 jit_solution(17908864913119374295)
XLA Ops:
  10.0 2.9 scatter_custom_fusion
  13.0 3.5 %gather_fusion = bf16[512]{0:T(512)(128)(2,1)S(1)} fusion(bf16[385]{0:T(512)(128)(2,1)S(1)} %pad_maximum_fusion.3, s32[1024]{0:T(1024)S(1)} %pad_clamp_fusion.2), kind=kCustom, calls=%fused_computation | custom fusion | bytes 4096 | tf_op jit(solution)/shard_map/gather | solution.py:68
  17.2 13.5 %all-to-all-start = ((bf16[64,1,8]{2,1,0:T(2,128)(2,1)}), bf16[64,1,8]{2,1,0:T(2,128)(2,1)S(1)}, u32[]{:S(2)}, u32[]{:S(2)}) async-start(bf16[64,1,8]{2,1,0:T(2,128)(2,1)} %all_to_all.25), calls=%async_computation | async-start | bytes 65536 | tf_op jit(solution)/shard_map/all_to_all | solution.py:78
  30.7 2.9 scatter_custom_fusion.1
  33.7 3.3 gather_fusion.2
  39.9 8.0 %all-to-all-start.2 = ((bf16[64,8,2048]{2,1,0:T(8,128)(2,1)}), bf16[64,8,2048]{2,1,0:T(8,128)(2,1)S(1)}, u32[]{:S(2)}, u32[]{:S(2)}) async-start(bf16[64,8,2048]{2,1,0:T(8,128)(2,1)} %bitcast.4), calls=%async_computation.2 | async-start | bytes 4194304 | tf_op jit(solution)/shard_map/all_to_all | solution.py:76
  48.7 3.3 gather_fusion.1
  51.9 44.9 %all-to-all-done.2 = bf16[64,8,2048]{2,1,0:T(8,128)(2,1)S(1)} async-done(((bf16[64,8,2048]{2,1,0:T(8,128)(2,1)}), bf16[64,8,2048]{2,1,0:T(8,128)(2,1)S(1)}, u32[]{:S(2)}, u32[]{:S(2)}) %all-to-all-start.2) | async-done | bytes 2097184 | tf_op jit(solution)/shard_map/all_to_all | solution.py:76
  98.2 7.6 %all-to-all-start.1 = ((bf16[64,8,2048]{2,1,0:T(8,128)(2,1)}), bf16[64,8,2048]{2,1,0:T(8,128)(2,1)S(1)}, u32[]{:S(2)}, u32[]{:S(2)}) async-start(bf16[64,8,2048]{2,1,0:T(8,128)(2,1)} %bitcast.1), calls=%async_computation.1 | async-start | bytes 4194304 | tf_op jit(solution)/shard_map/all_to_all | solution.py:77
  106.1 8.5 %fusion.2 = f32[512,1536]{1,0:T(8,128)} fusion(bf16[1,2048,1536]{2,1,0:T(8,128)(2,1)} %all-gather.5.cloned.1.call-done, bf16[64,8,2048]{2,1,0:T(8,128)(2,1)} %copy-done), kind=kOutput, calls=%fused_computation.10 | convolution fusion | flops 3221225472 | bytes 11534336 | tf_op jit(solution)/shard_map/dot_general | solution.py:13
  114.6 40.2 %all-to-all-done.1 = bf16[64,8,2048]{2,1,0:T(8,128)(2,1)S(1)} async-done(((bf16[64,8,2048]{2,1,0:T(8,128)(2,1)}), bf16[64,8,2048]{2,1,0:T(8,128)(2,1)S(1)}, u32[]{:S(2)}, u32[]{:S(2)}) %all-to-all-start.1) | async-done | bytes 2097184 | tf_op jit(solution)/shard_map/all_to_all | solution.py:77
  154.8 5.3 %multiply_convert_fusion.2 = (bf16[512,768]{1,0:T(8,128)(2,1)S(1)}, bf16[512,768]{1,0:T(8,128)(2,1)S(1)}, bf16[512,768]{1,0:T(8,128)(2,1)S(1)}) fusion(f32[512,1536]{1,0:T(8,128)} %fusion.2, bf16[1,768,2048]{2,1,0:T(8,128)(2,1)} %all-gather.3.cloned.1.call-done, bf16[64,8,2048]{2,1,0:T(8,128)(2,1)S(1)} %all-to-all-done.1, f32[64,8]{1,0:T(8,128)S(1)} %bitcast.54), kind=kOutput, calls=%fused_computation.35 | convolution fusion | flops 1619656704 | bytes 10749952 | tf_op jit(solution)/shard_map/dot_general | solution.py:29
  161.3 5.5 %convolution_convert_fusion = bf16[2048,1536]{1,0:T(8,128)(2,1)} fusion(bf16[64,8,2048]{2,1,0:T(8,128)(2,1)S(1)} %copy-done.1, bf16[512,768]{1,0:T(8,128)(2,1)S(1)} %get-tuple-element.13, bf16[512,768]{1,0:T(8,128)(2,1)S(1)} %get-tuple-element.12), kind=kOutput, calls=%fused_computation.7 | convolution fusion | flops 3227516928 | bytes 9961472 | tf_op jit(solution)/shard_map/dot_general | solution.py:111
  167.1 3.6 %convolution_convert_fusion.1 = bf16[768,2048]{1,0:T(8,128)(2,1)} fusion(bf16[512,768]{1,0:T(8,128)(2,1)S(1)} %get-tuple-element.14, bf16[64,8,2048]{2,1,0:T(8,128)(2,1)S(1)} %all-to-all-done.1, f32[512]{0:T(512)S(1)} %reshape.123), kind=kOutput, calls=%fused_computation.19 | convolution fusion | flops 1615331328 | bytes 6031360 | tf_op jit(solution)/shard_map/dot_general | solution.py:123
  170.7 3.8 %fusion.6 = bf16[512]{0:T(512)(128)(2,1)S(1)} fusion(bf16[64,8,2048]{2,1,0:T(8,128)(2,1)S(1)} %all-to-all-done.1, bf16[512,768]{1,0:T(8,128)(2,1)S(1)} %get-tuple-element.14, bf16[1,768,2048]{2,1,0:T(8,128)(2,1)} %all-gather.3.cloned.1.call-done), kind=kOutput, calls=%fused_computation.16 | convolution fusion | flops 1613757952 | bytes 6030336 | tf_op jit(solution)/shard_map/dot_general | solution.py:19
  175.2 7.7 %all-to-all-start.4 = ((bf16[64,1,8]{2,1,0:T(2,128)(2,1)}), bf16[64,1,8]{2,1,0:T(2,128)(2,1)S(1)}, u32[]{:S(2)}, u32[]{:S(2)}) async-start(bf16[64,1,8]{2,1,0:T(2,128)(2,1)} %convert_element_type.135), calls=%async_computation.4 | async-start | bytes 65536 | tf_op jit(solution)/shard_map/all_to_all | solution.py:95
  183.0 8.4 %fusion.15 = bf16[64,8,2048]{2,1,0:T(8,128)(2,1)} fusion(bf16[1,2048,1536]{2,1,0:T(8,128)(2,1)} %all-gather.5.cloned.1.call-done, bf16[512,768]{1,0:T(8,128)(2,1)} %copy-done.8, bf16[512,768]{1,0:T(8,128)(2,1)} %copy-done.7), kind=kOutput, calls=%fused_computation.25 | convolution fusion | flops 3225419776 | bytes 9961472 | tf_op jit(solution)/shard_map/dot_general | solution.py:37
  191.9 10.1 %all-to-all-start.3 = ((bf16[64,8,2048]{2,1,0:T(8,128)(2,1)}), bf16[64,8,2048]{2,1,0:T(8,128)(2,1)S(1)}, u32[]{:S(2)}, u32[]{:S(2)}) async-start(bf16[64,8,2048]{2,1,0:T(8,128)(2,1)} %fusion.15), calls=%async_computation.3 | async-start | bytes 4194304 | tf_op jit(solution)/shard_map/all_to_all | solution.py:88
  202.1 56.5 %reduce-scatter.3.cloned.1.call-done = bf16[512,1536]{1,0:T(8,128)(2,1)} async-done(((bf16[2048,1536]{1,0:T(8,128)(2,1)}), bf16[512,1536]{1,0:T(8,128)(2,1)}) %reduce-scatter.3.cloned.1.call-update) | async-done | bytes 1572880 | tf_op jit(solution)/shard_map/reduce_scatter | solution.py:114
  261.3 50.2 %reduce-scatter.5.cloned.1.call-done = bf16[192,2048]{1,0:T(8,128)(2,1)} async-done(((bf16[768,2048]{1,0:T(8,128)(2,1)}), bf16[192,2048]{1,0:T(8,128)(2,1)}) %reduce-scatter.5.cloned.1.call-update) | async-done | bytes 786448 | tf_op jit(solution)/shard_map/reduce_scatter | solution.py:126
  319.4 3.1 gather_fusion.3
  322.5 5.5 %reshape.120 = f32[128,3,2048]{2,1,0:T(4,128)} reshape(bf16[384,2048]{1,0:T(8,128)(2,1)} %gather_fusion.3) | data formatting | bytes 4718592 | tf_op jit(solution)/shard_map/convert_element_type | solution.py:105
  328.0 5.9 %reduce_sum.27 = f32[128,2048]{1,0:T(8,128)} reduce(f32[128,3,2048]{2,1,0:T(4,128)} %reshape.120, f32[]{:T(128)} %constant.14.clone.1), dimensions={1}, to_apply=%region_2.3 | reduce | flops 524288 | bytes 4194308 | tf_op jit(solution)/shard_map/reduce_sum | solution.py:104
  335.9 3.5 %convert_select_fusion = f32[1,512,1536]{2,1,0:T(8,128)} fusion(bf16[1,512,1536]{2,1,0:T(8,128)(2,1)} %collective-permute-done, pred[]{:T(512)S(6)} %eq.12, bf16[512,1536]{1,0:T(8,128)(2,1)S(1)} %copy-done.2), kind=kLoop, calls=%fused_computation.23 | loop fusion | flops 2359296 | bytes 6291457 | tf_op jit(solution)/shard_map/jit(_where)/select_n | solution.py:138
  (64 shorter events, 23.4 us)
Async XLA Ops:
  7.2 26.5 %copy-start.4 = (bf16[128,2048]{1,0:T(8,128)(2,1)S(1)}, bf16[128,2048]{1,0:T(8,128)(2,1)}, u32[]{:S(2)}) copy-start(bf16[128,2048]{1,0:T(8,128)(2,1)} %param.8) | copy-start | bytes 1572868
  7.2 98.9 %all-gather.5.cloned.1.call-start = ((), (), s32[]{:S(2)}) async-start(), calls=%async_computation.8 | async-start | bytes 7864320 | tf_op jit(solution)/shard_map/all_gather | solution.py:70
  17.2 22.6 %all-to-all-start = ((bf16[64,1,8]{2,1,0:T(2,128)(2,1)}), bf16[64,1,8]{2,1,0:T(2,128)(2,1)S(1)}, u32[]{:S(2)}, u32[]{:S(2)}) async-start(bf16[64,1,8]{2,1,0:T(2,128)(2,1)} %all_to_all.25), calls=%async_computation | async-start | bytes 65536 | tf_op jit(solution)/shard_map/all_to_all | solution.py:78
  39.9 8.7 %copy-start.5 = (bf16[128,2048]{1,0:T(8,128)(2,1)S(1)}, bf16[128,2048]{1,0:T(8,128)(2,1)}, u32[]{:S(2)}) copy-start(bf16[128,2048]{1,0:T(8,128)(2,1)} %param.9) | copy-start | bytes 1572868
  39.9 57.0 %all-to-all-start.2 = ((bf16[64,8,2048]{2,1,0:T(8,128)(2,1)}), bf16[64,8,2048]{2,1,0:T(8,128)(2,1)S(1)}, u32[]{:S(2)}, u32[]{:S(2)}) async-start(bf16[64,8,2048]{2,1,0:T(8,128)(2,1)} %bitcast.4), calls=%async_computation.2 | async-start | bytes 4194304 | tf_op jit(solution)/shard_map/all_to_all | solution.py:76
  47.8 107.0 %all-gather.3.cloned.1.call-start = ((), (), s32[]{:S(2)}) async-start(), calls=%async_computation.7 | async-start | bytes 3932160 | tf_op jit(solution)/shard_map/all_gather | solution.py:71
  96.8 1.3 copy-start
  98.2 56.6 %all-to-all-start.1 = ((bf16[64,8,2048]{2,1,0:T(8,128)(2,1)}), bf16[64,8,2048]{2,1,0:T(8,128)(2,1)S(1)}, u32[]{:S(2)}, u32[]{:S(2)}) async-start(bf16[64,8,2048]{2,1,0:T(8,128)(2,1)} %bitcast.1), calls=%async_computation.1 | async-start | bytes 4194304 | tf_op jit(solution)/shard_map/all_to_all | solution.py:77
  105.8 152.8 %reduce-scatter.3.cloned.1.call-start = ((), (), s32[]{:S(2)}) async-start(), calls=%async_computation.9 | async-start | bytes 7864320 | tf_op jit(solution)/shard_map/reduce_scatter | solution.py:114
  154.8 6.4 %copy-start.1 = (bf16[64,8,2048]{2,1,0:T(8,128)(2,1)S(1)}, bf16[64,8,2048]{2,1,0:T(8,128)(2,1)}, u32[]{:S(2)}) copy-start(bf16[64,8,2048]{2,1,0:T(8,128)(2,1)} %copy-done) | copy-start | bytes 6291460
  160.1 0.9 copy-start.7
  160.2 1.1 copy-start.8
  166.8 144.7 %reduce-scatter.5.cloned.1.call-start = ((), (), s32[]{:S(2)}) async-start(), calls=%async_computation.10 | async-start | bytes 3932160 | tf_op jit(solution)/shard_map/reduce_scatter | solution.py:126
  175.2 16.7 %all-to-all-start.4 = ((bf16[64,1,8]{2,1,0:T(2,128)(2,1)}), bf16[64,1,8]{2,1,0:T(2,128)(2,1)S(1)}, u32[]{:S(2)}, u32[]{:S(2)}) async-start(bf16[64,1,8]{2,1,0:T(2,128)(2,1)} %convert_element_type.135), calls=%async_computation.4 | async-start | bytes 65536 | tf_op jit(solution)/shard_map/all_to_all | solution.py:95
  191.4 122.8 %copy-start.6 = (s32[64]{0:T(128)S(1)}, s32[64]{0:T(128)}, u32[]{:S(2)}) copy-start(s32[64]{0:T(128)} %param.13) | copy-start | bytes 772
  191.9 127.5 %all-to-all-start.3 = ((bf16[64,8,2048]{2,1,0:T(8,128)(2,1)}), bf16[64,8,2048]{2,1,0:T(8,128)(2,1)S(1)}, u32[]{:S(2)}, u32[]{:S(2)}) async-start(bf16[64,8,2048]{2,1,0:T(8,128)(2,1)} %fusion.15), calls=%async_computation.3 | async-start | bytes 4194304 | tf_op jit(solution)/shard_map/all_to_all | solution.py:88
  258.6 76.6 %collective-permute-start = (bf16[1,512,1536]{2,1,0:T(8,128)(2,1)}, bf16[1,512,1536]{2,1,0:T(8,128)(2,1)}, u32[]{:S(2)}, u32[]{:S(2)}) collective-permute-start(bf16[1,512,1536]{2,1,0:T(8,128)(2,1)} %bitcast.52), channel_id=1, source_target_pairs={{0,32},{1,33},{2,34},{3,35},{4,36},{5,37},{6,38},{7,39},{8,40},{9,... | collective-permute-start | bytes 4718600 | tf_op jit(solution)/shard_map/ppermute | solution.py:8
  311.6 22.3 %collective-permute-start.1 = (bf16[1,192,2048]{2,1,0:T(8,128)(2,1)}, bf16[1,192,2048]{2,1,0:T(8,128)(2,1)S(1)}, u32[]{:S(2)}, u32[]{:S(2)}) collective-permute-start(bf16[1,192,2048]{2,1,0:T(8,128)(2,1)} %bitcast.53), channel_id=1, source_target_pairs={{0,32},{1,33},{2,34},{3,35},{4,36},{5,37},{6,38},{7,39},{8,40},{9,... | collective-permute-start | bytes 2359304 | tf_op jit(solution)/shard_map/ppermute | solution.py:8
  328.0 5.9 %copy-start.3 = (bf16[192,2048]{1,0:T(8,128)(2,1)S(1)}, bf16[192,2048]{1,0:T(8,128)(2,1)}, u32[]{:S(2)}) copy-start(bf16[192,2048]{1,0:T(8,128)(2,1)} %reduce-scatter.5.cloned.1.call-done) | copy-start | bytes 2359300
  333.9 2.0 copy-start.2
Sparse Core Ops, SparseCore 0:
  9.8 70.6 all-gather.4
  82.3 45.8 all-gather.2
  167.0 91.6 reduce-scatter.2
  262.1 49.4 reduce-scatter.4
where the time goes:
time: 347 us; the launch traced here: 346 us
  waiting for transfers between devices  197 us (57%)
  starting transfers between devices  52.6 us (15%)
  matrix products  35.2 us (10%)
  local copies, waits for them, and re-layouts  33.6 us (10%)
  between operations  14.7 us (4%)
  other arithmetic  13.1 us (4%)
    reduce_scatter x2, waiting for transfers between devices, body(): lax.psum_scatter(lax.optimization_barrier(term.astype(jnp.bfloat16)).asty...  107 us
    all_to_all x1, waiting for transfers between devices, body(): lax.all_to_all(send_rows, 'expert', split_axis=0, concat_axis=0, tiled=True)  44.9 us
    all_to_all x1, waiting for transfers between devices, body(): lax.all_to_all(send_cot, 'expert', split_axis=0, concat_axis=0, tiled=True)  40.2 us
    all_to_all x1, starting transfers between devices, body(): lax.all_to_all(send_weight, 'expert', split_axis=0, concat_axis=0, tiled=...  13.5 us
    all_to_all x1, starting transfers between devices, body(): lax.all_to_all(row_grad.reshape(count_dev, capacity, model_width), 'exper...  10.1 us
    dot_general x1, matrix products, forward_pass(): gate_up = jnp.dot(rows_in, gate_up_w, preferred_element_type=jnp.float32)  8.53 us
    dot_general x1, matrix products, backward_pass(): lax.dot_general(both_grad, gate_up_w, (((1,), (1,)), ((), ())), preferred...  8.44 us
    all_to_all x1, starting transfers between devices, body(): lax.all_to_all(send_rows, 'expert', split_axis=0, concat_axis=0, tiled=True)  7.98 us
  transfers between devices with their start and end apart: 11, of which 6 were waited for; matrix products, arithmetic and copies ran while one was open for 18% of the time, Pallas kernels for 0%

commit v1 on v0

v1 whole, which is shorter than its diff:
```python
import functools

import jax
import jax.numpy as jnp
from jax import lax
from jax.experimental import pallas as pl
from jax.experimental.pallas import tpu as pltpu
from jax.sharding import PartitionSpec as P

BF = jnp.bfloat16
F32 = jnp.float32
MESH = pl.DeviceIdType.MESH
GROUPS = 4
SLOTS = 8
LANES = 128
VMEM_BYTES = 60 * 2**20

ROWS_BY_ROWS = (((1,), (1,)), ((), ()))
COLS_BY_COLS = (((0,), (0,)), ((), ()))


def pick_tile(width, largest):
    tile = min(width, largest)
    while width % tile:
        tile -= LANES
    return tile


def exchange_kernel(
    sizes, hr_ref, idx_ref, weight_ref, flag_ref, tok_ref, cot_ref, wg_ref, wd_ref,
    ret_ref, own_g, own_d, far_g, far_d,
    sendb, recvb, mig_g, mig_d, full_g, full_d, rows_b, scaled_b, hid_b, both_b,
    retb, part_g, part_d, sib_g, sib_d,
    a2a_send, a2a_recv, ret_send, ret_recv,
    mig_send, mig_recv, far_send, far_recv, sib_send, sib_recv, fwd_send, fwd_recv,
    red_send, red_recv, out_send, out_recv,
):
    experts, width, ff = sizes
    block = experts // GROUPS
    chunk = block * SLOTS
    half = width // 2
    quarter_g, quarter_d = width // 4, ff // 4
    dp = lax.axis_index("dp")
    me = lax.axis_index("expert")
    my_group = me // block
    sib, far = dp ^ 1, dp ^ 2

    def remote(src, dst, send, recv, where):
        return pltpu.make_async_remote_copy(
            src_ref=src, dst_ref=dst, send_sem=send, recv_sem=recv,
            device_id=where, device_id_type=MESH,
        )

    step = quarter_g // 4
    pieces = [(True, k * step, step) for k in range(4)] + [(False, 0, quarter_d)]
    swaps = []
    for k, (is_g, off, count) in enumerate(pieces):
        src, dst = (wg_ref, mig_g) if is_g else (wd_ref, mig_d)
        copy = remote(
            src.at[pl.ds(off, count)], dst.at[pl.ds(off, count)],
            mig_send.at[k], mig_recv.at[k], (dp, me ^ (experts // 2)),
        )
        copy.start()
        swaps.append(copy)

    prep_tile = pick_tile(width, 512)

    def dispatch(g, carry):
        first = (my_group ^ g) * block
        codes = hr_ref[pl.ds(pl.multiple_of(first * SLOTS, SLOTS), chunk), :]
        pick = jnp.zeros((chunk, idx_ref.shape[1]), F32)
        pick_w = jnp.zeros((chunk, idx_ref.shape[1]), F32)
        for k in range(3):
            hit = codes == idx_ref[k : k + 1, :]
            pick = jnp.where(hit, 1.0, pick)
            pick_w = jnp.where(hit, weight_ref[k : k + 1, :], pick_w)
        pick = pick.astype(BF)
        pick_w = pick_w.astype(BF)
        for c in range(0, width, prep_tile):
            cols = slice(c, c + prep_tile)
            rows = jnp.dot(pick, tok_ref[:, cols], preferred_element_type=F32)
            cots = jnp.dot(pick_w, cot_ref[:, cols], preferred_element_type=F32)
            both = jnp.concatenate(
                [rows.reshape(block, SLOTS, prep_tile), cots.reshape(block, SLOTS, prep_tile)],
                axis=1,
            )
            sendb[pl.ds(first, block), :, cols] = both.astype(BF)

        def send(i, carry):
            peer = me ^ (g * block + i)

            @pl.when(peer != me)
            def _():
                remote(
                    sendb.at[peer], recvb.at[me], a2a_send, a2a_recv.at[g], (dp, peer)
                ).start()

            @pl.when(peer == me)
            def _():
                pltpu.make_async_copy(sendb.at[me], recvb.at[me], a2a_recv.at[g]).start()

            return carry

        return lax.fori_loop(0, block, send, carry)

    lax.fori_loop(0, GROUPS, dispatch, 0)

    lane = lax.broadcasted_iota(jnp.int32, flag_ref.shape, 1)
    mine = jnp.where(lane == me, flag_ref[...], 0)
    flagged = jnp.max(mine, axis=1, keepdims=True) == 1
    fars, sibs = [], []
    for k, (is_g, off, count) in enumerate(pieces):
        swaps[k].wait_recv()
        if is_g:
            own, mig, full, quarter = wg_ref, mig_g, full_g, quarter_g
        else:
            own, mig, full, quarter = wd_ref, mig_d, full_d, quarter_d
        chosen = jnp.where(flagged, mig[pl.ds(off, count), :], own[pl.ds(off, count), :])
        place = pl.ds(pl.multiple_of(dp * quarter + off, 16), count)
        full[place, :] = chosen
        copy = remote(full.at[place], full.at[place], far_send.at[k], far_recv.at[k], (far, me))
        copy.start()
        fars.append(copy)
        copy = remote(full.at[place], full.at[place], sib_send.at[k], sib_recv.at[k], (sib, me))
        copy.start()
        sibs.append(copy)
    fwds = []
    for k, (is_g, off, count) in enumerate(pieces):
        fars[k].wait_recv()
        full, quarter = (full_g, quarter_g) if is_g else (full_d, quarter_d)
        place = pl.ds(pl.multiple_of(far * quarter + off, 16), count)
        copy = remote(full.at[place], full.at[place], fwd_send.at[k], fwd_recv.at[k], (sib, me))
        copy.start()
        fwds.append(copy)
    for k in range(len(pieces)):
        sibs[k].wait_recv()
        fwds[k].wait_recv()

    ff_tile = pick_tile(ff, 256)
    half_tile = pick_tile(half, 256)

    def expert(g, carry):
        first = (my_group ^ g) * block
        arrived = recvb.at[pl.ds(first, block)]
        pltpu.make_async_copy(arrived, arrived, a2a_recv.at[g]).wait()
        place = pl.ds(pl.multiple_of(g * chunk, chunk), chunk)
        for c in range(0, width, prep_tile):
            cols = slice(c, c + prep_tile)
            both = recvb[pl.ds(first, block), :, cols].astype(F32)
            rows_b[place, cols] = both[:, :SLOTS].reshape(chunk, prep_tile).astype(BF)
            scaled_b[place, cols] = both[:, SLOTS:].reshape(chunk, prep_tile).astype(BF)
        prob = jnp.zeros((chunk, 1), F32)
        for f in range(0, ff, ff_tile):
            cols = slice(f, f + ff_tile)
            up_cols = slice(ff + f, ff + f + ff_tile)
            rows = rows_b[place, :]
            gate = jnp.dot(rows, full_g[:, cols], preferred_element_type=F32)
            up = jnp.dot(rows, full_g[:, up_cols], preferred_element_type=F32)
            hgrad = lax.dot_general(
                scaled_b[place, :], full_d[cols, :], ROWS_BY_ROWS, preferred_element_type=F32
            )
            sig = jax.nn.sigmoid(gate)
            silu = gate * sig
            hid = (silu * up).astype(BF)
            hid_b[place, cols] = hid
            both_b[place, cols] = (hgrad * up * sig * (1.0 + gate * (1.0 - sig))).astype(BF)
            both_b[place, up_cols] = (hgrad * silu).astype(BF)
            prob = prob + jnp.sum(hid.astype(F32) * hgrad, axis=1, keepdims=True)
        for c in range(0, half, half_tile):
            lo = lax.dot_general(
                both_b[place, :], full_g[c : c + half_tile, :], ROWS_BY_ROWS,
                preferred_element_type=F32,
            )
            hi = lax.dot_general(
                both_b[place, :], full_g[half + c : half + c + half_tile, :], ROWS_BY_ROWS,
                preferred_element_type=F32,
            )
            both = jnp.concatenate(
                [lo.reshape(block, SLOTS, half_tile), hi.reshape(block, SLOTS, half_tile)], axis=1
            )
            retb[pl.ds(first, block), :, c : c + half_tile] = both.astype(BF)
        prob = jnp.broadcast_to(prob, (chunk, LANES))
        rough = prob.astype(BF).astype(F32)
        both = jnp.concatenate(
            [rough.reshape(block, SLOTS, LANES), (prob - rough).reshape(block, SLOTS, LANES)],
            axis=1,
        )
        retb[pl.ds(first, block), :, half : half + LANES] = both.astype(BF)

        def send(i, carry):
            peer = me ^ (g * block + i)

            @pl.when(peer != me)
            def _():
                remote(retb.at[peer], ret_ref.at[me], ret_send, ret_recv, (dp, peer)).start()

            @pl.when(peer == me)
            def _():
                pltpu.make_async_copy(retb.at[me], ret_ref.at[me], ret_recv).start()

            return carry

        return lax.fori_loop(0, block, send, carry)

    lax.fori_loop(0, GROUPS, expert, 0)

    wide = pick_tile(2 * ff, 768)
    d_tile = pick_tile(quarter_g, 256)

    def gate_up_grads(quarter):
        def tile(i, carry):
            start = pl.multiple_of(quarter * quarter_g + i * d_tile, d_tile)
            left = rows_b[:, pl.ds(start, d_tile)]
            for c in range(0, 2 * ff, wide):
                part_g[pl.ds(start, d_tile), c : c + wide] = lax.dot_general(
                    left, both_b[:, c : c + wide], COLS_BY_COLS, preferred_element_type=F32
                ).astype(BF)
            return carry

        lax.fori_loop(0, quarter_g // d_tile, tile, 0)

    def down_grads():
        for f in range(0, ff, ff_tile):
            for c in range(0, width, prep_tile):
                part_d[f : f + ff_tile, c : c + prep_tile] = lax.dot_general(
                    hid_b[:, f : f + ff_tile], scaled_b[:, c : c + prep_tile], COLS_BY_COLS,
                    preferred_element_type=F32,
                ).astype(BF)

    def place_of(quarter, rows):
        return pl.ds(pl.multiple_of(quarter * rows, 16), rows)

    reds = []

    def to_sibling(slot, part, rows, landing, quarter):
        copy = remote(
            part.at[place_of(quarter, rows)], landing.at[slot % 2],
            red_send.at[slot], red_recv.at[slot], (sib, me),
        )
        copy.start()
        reds.append(copy)

    outs = []

    def to_far(slot, part, rows, landing, out):
        reds[slot].wait_recv()
        total = part[place_of(far, rows), :].astype(F32) + landing[0].astype(F32)
        landing[0] = total.astype(BF)
        copy = remote(landing.at[0], out, out_send.at[slot // 2], out_recv.at[slot // 2], (far, me))
        copy.start()
        outs.append(copy)

    gate_up_grads(far ^ 1)
    to_sibling(0, part_g, quarter_g, sib_g, far ^ 1)
    gate_up_grads(far)
    to_far(0, part_g, quarter_g, sib_g, far_g)
    gate_up_grads(dp ^ 1)
    to_sibling(1, part_g, quarter_g, sib_g, dp ^ 1)
    down_grads()
    to_sibling(2, part_d, quarter_d, sib_d, far ^ 1)
    to_far(2, part_d, quarter_d, sib_d, far_d)
    to_sibling(3, part_d, quarter_d, sib_d, dp ^ 1)
    gate_up_grads(dp)
    reds[1].wait_recv()
    own_g[...] = (
        part_g[place_of(dp, quarter_g), :].astype(F32) + sib_g[1].astype(F32)
    ).astype(BF)
    reds[3].wait_recv()
    own_d[...] = (
        part_d[place_of(dp, quarter_d), :].astype(F32) + sib_d[1].astype(F32)
    ).astype(BF)

    others = sendb.at[pl.ds(0, experts - 1)]
    pltpu.make_async_copy(others, others, a2a_send).wait()
    for copy in swaps + fars + sibs + fwds + reds:
        copy.wait_send()
    others = retb.at[pl.ds(0, experts - 1)]
    pltpu.make_async_copy(others, others, ret_send).wait()
    pltpu.make_async_copy(retb, retb, ret_recv).wait()
    for copy in outs:
        copy.wait()


def combine_kernel(ret_ref, idx_ref, weight_ref, hr_ref, tok_out, weight_out):
    experts, _, cols = ret_ref.shape
    half = cols - LANES
    rows = experts * SLOTS
    hits = [hr_ref[0:1, :] == idx_ref[:, k : k + 1] for k in range(3)]
    pick = jnp.zeros(hits[0].shape, F32)
    for hit in hits:
        pick = jnp.where(hit, 1.0, pick)
    pick = pick.astype(BF)
    tile = pick_tile(half, 512)
    for c in range(0, half, tile):
        both = ret_ref[:, :, c : c + tile].astype(F32)
        lo = both[:, :SLOTS].reshape(rows, tile).astype(BF)
        hi = both[:, SLOTS:].reshape(rows, tile).astype(BF)
        tok_out[:, c : c + tile] = jnp.dot(pick, lo, preferred_element_type=F32)
        tok_out[:, half + c : half + c + tile] = jnp.dot(pick, hi, preferred_element_type=F32)
    both = ret_ref[:, :, half:].astype(F32)
    rough = both[:, :SLOTS].reshape(rows, LANES).astype(BF)
    rest = both[:, SLOTS:].reshape(rows, LANES).astype(BF)
    for k in range(3):
        one = jnp.where(hits[k], 1.0, 0.0).astype(BF)
        prob = jnp.dot(one, rough, preferred_element_type=F32)
        prob = prob + jnp.dot(one, rest, preferred_element_type=F32)
        weight_out[:, k : k + 1] = prob[:, 0:1] / weight_ref[:, k : k + 1]


def body(tokens, cotangent, routes, slot_index, route_weight, swap_flags, w_gate_up, w_down):
    tok_rows, width = tokens.shape
    experts = swap_flags.shape[0]
    ff = w_down.shape[1] * lax.axis_size("dp")
    rows = experts * SLOTS
    quarter_g, quarter_d = w_gate_up.shape[1], w_down.shape[1]
    pieces = 5

    idx = routes * SLOTS + slot_index
    weight = route_weight.astype(BF).astype(F32)
    hr = jnp.arange(rows, dtype=jnp.int32) ^ (jnp.repeat(swap_flags, SLOTS) * (rows // 2))

    vmem = pl.BlockSpec(memory_space=pltpu.VMEM)
    hbm = pl.BlockSpec(memory_space=pl.ANY)
    dma = pltpu.SemaphoreType.DMA
    flops = 2 * rows * width * ff * 9
    ret, own_g, own_d, far_g, far_d = pl.pallas_call(
        functools.partial(exchange_kernel, (experts, width, ff)),
        name="exchange",
        out_shape=(
            jax.ShapeDtypeStruct((experts, 2 * SLOTS, width // 2 + LANES), BF),
            jax.ShapeDtypeStruct((quarter_g, 2 * ff), BF),
            jax.ShapeDtypeStruct((quarter_d, width), BF),
            jax.ShapeDtypeStruct((quarter_g, 2 * ff), BF),
            jax.ShapeDtypeStruct((quarter_d, width), BF),
        ),
        in_specs=[vmem] * 8,
        out_specs=(hbm, vmem, vmem, hbm, hbm),
        scratch_shapes=[
            pltpu.VMEM((experts, 2 * SLOTS, width), BF),
            pltpu.VMEM((experts, 2 * SLOTS, width), BF),
            pltpu.VMEM((quarter_g, 2 * ff), BF),
            pltpu.VMEM((quarter_d, width), BF),
            pltpu.VMEM((width, 2 * ff), BF),
            pltpu.VMEM((ff, width), BF),
            pltpu.VMEM((rows, width), BF),
            pltpu.VMEM((rows, width), BF),
            pltpu.VMEM((rows, ff), BF),
            pltpu.VMEM((rows, 2 * ff), BF),
            pltpu.VMEM((experts, 2 * SLOTS, width // 2 + LANES), BF),
            pltpu.VMEM((width, 2 * ff), BF),
            pltpu.VMEM((ff, width), BF),
            pltpu.VMEM((2, quarter_g, 2 * ff), BF),
            pltpu.VMEM((2, quarter_d, width), BF),
            dma, dma((GROUPS,)), dma, dma,
            dma((pieces,)), dma((pieces,)), dma((pieces,)), dma((pieces,)),
            dma((pieces,)), dma((pieces,)), dma((pieces,)), dma((pieces,)),
            dma((4,)), dma((4,)), dma((2,)), dma((2,)),
        ],
        compiler_params=pltpu.CompilerParams(
            has_side_effects=True, vmem_limit_bytes=VMEM_BYTES
        ),
        cost_estimate=pl.CostEstimate(
            flops=flops, bytes_accessed=12 * 2**20, transcendentals=rows * ff
        ),
    )(
        hr[:, None], idx.T, weight.T, swap_flags[None], tokens, cotangent, w_gate_up[0], w_down[0]
    )

    grad_tokens, grad_weight = pl.pallas_call(
        combine_kernel,
        name="combine",
        out_shape=(
            jax.ShapeDtypeStruct((tok_rows, width), F32),
            jax.ShapeDtypeStruct((tok_rows, 3), F32),
        ),
        in_specs=[vmem] * 4,
        out_specs=(vmem, vmem),
        compiler_params=pltpu.CompilerParams(vmem_limit_bytes=32 * 2**20),
    )(ret, idx, weight, hr[None])
    grad_gu = (own_g.astype(F32) + far_g.astype(F32))[None]
    grad_dn = (own_d.astype(F32) + far_d.astype(F32))[None]
    return (grad_tokens, grad_weight, grad_gu, grad_dn)


def solution(mesh):
    return jax.shard_map(
        body,
        mesh=mesh,
        in_specs=(
            P(("dp", "expert"), None),
            P(("dp", "expert"), None),
            P(("dp", "expert"), None),
            P(("dp", "expert"), None),
            P(("dp", "expert"), None),
            P(),
            P("expert", "dp", None),
            P("expert", "dp", None),
        ),
        out_specs=(
            P(("dp", "expert"), None),
            P(("dp", "expert"), None),
            P("expert", "dp", None),
            P("expert", "dp", None),
        ),
        check_vma=False,
    )
```

time: 347 us -> 256 us (0.74)
  Pallas kernels: 0 us -> 244 us
  waiting for transfers between devices: 197 us -> 0 us
  starting transfers between devices: 52.6 us -> 0 us
  matrix products: 35.2 us -> 0 us
  local copies, waits for them, and re-layouts: 33.6 us -> 4.58 us
  between operations: 14.7 us -> 0.68 us
  other arithmetic: 13.1 us -> 6.27 us
    pallas_call x0 -> x2, Pallas kernels: none -> 244 us  [the longest x1 242 us: body(): pl.pallas_call(functools.partial(exchange_kernel, (experts, width, ff)),...]
    reduce_scatter x2 -> x0, waiting for transfers between devices: 107 us -> none  [body(): lax.psum_scatter(lax.optimization_barrier(term.astype(jnp.bfloat16)).asty...]
    all_to_all x5 -> x0, waiting for transfers between devices: 88.5 us -> none  [the longest x1 44.9 us: body(): lax.all_to_all(send_rows, 'expert', split_axis=0, concat_axis=0, tiled=True)]
    all_to_all x5 -> x0, starting transfers between devices: 46.9 us -> none  [the longest x1 13.5 us: body(): lax.all_to_all(send_weight, 'expert', split_axis=0, concat_axis=0, tiled=...]
    dot_general x6 -> x0, matrix products: 35.2 us -> none  [the longest x1 8.53 us: forward_pass(): gate_up = jnp.dot(rows_in, gate_up_w, preferred_element_type=jnp.float32)]
    gather x5 -> x0, local copies, waits for them, and re-layouts: 16 us -> none  [the longest x1 3.51 us: body(): send_weight = weight_flat[assign_of_row].reshape(count_dev, capacity)]
    reduce_sum x2 -> x0, other arithmetic: 6.51 us -> none  [the longest x1 5.88 us: body(): jnp.sum(picked_rows.astype(jnp.float32).reshape(tok_rows, top_count, mode...]
    convert_element_type x5 -> x1, local copies, waits for them, and re-layouts: 6.62 us -> 0.13 us  [body(): weight = route_weight.astype(BF).astype(F32)]
  transfers between devices with their start and end apart: 11 -> 0, of which waited for: 6 -> 0; matrix products, arithmetic and copies ran while one was open for 18% -> 0% of each run, Pallas kernels for 0% -> 0%
where the time goes in v1:
time: 256 us; the launch traced here: 255 us
  Pallas kernels  244 us (95%)
  other arithmetic  6.27 us (2%)
  local copies, waits for them, and re-layouts  4.58 us (2%)
    pallas_call x1, Pallas kernels, body(): pl.pallas_call(functools.partial(exchange_kernel, (experts, width, ff)),...  242 us

profile of v1, /device:TPU:1, one launch (start us, length us, event | category | flops | bytes accessed | tf_op | source)
XLA Modules:
  0.0 255.2 jit_solution(9239918443183620055)
XLA Ops:
  0.6 0.7 broadcast_multiply_fusion
  1.3 0.7 convert_element_type.18
  2.0 0.7 multiply_add_fusion
  2.7 0.1 copy.28
  2.8 0.1 broadcast_in_dim.14
  2.9 0.1 mul.39
  3.0 0.1 copy.30.idx_ref
  3.1 0.7 copy.29.weight_ref
  3.8 0.1 mul.40
  3.9 0.7 iota_xor_fusion.hr_ref
  4.6 0.0 copy-done.5
  4.6 242.2 %exchange.1 = (bf16[64,16,1152]{2,1,0:T(8,128)(2,1)}, bf16[512,1536]{1,0:T(8,128)(2,1)}, bf16[192,2048]{1,0:T(8,128)(2,1)}, bf16[512,1536]{1,0:T(8,128)(2,1)}, bf16[192,2048]{1,0:T(8,128)(2,1)}) custom-call(s32[512,1]{1,0:T(8,128)} %iota_xor_fusion.hr_ref, s32[3,128]{1,0:T(4,128)} %bitcast.10, f32[3,128]{1,0:T(4,128)} %copy.29.weight_ref, s32[1,64]{1,0:T(1,128)} %bitcast.13, ...), custom_call_target="tpu_custom_call" | custom-call | flops 14495514624 | bytes 12582912 | tf_op jit(solution)/shard_map/exchange/pallas_call | solution.py:326
  246.8 0.0 copy-start
  246.9 1.7 copy-done
  248.5 0.0 copy-start.3
  248.5 0.0 copy-start.4
  248.5 1.5 combine.1
  250.0 0.7 copy.31
  250.7 0.0 copy-done.3
  250.7 0.0 copy-done.4
  250.7 1.4 add_bitcast_fusion.1
  252.0 0.6 copy-done.1
  252.6 0.5 copy-done.2
  253.1 2.1 add_bitcast_fusion
  (5 shorter events, 0.0 us)
Async XLA Ops:
  2.7 2.0 copy-start.5
  246.8 1.7 copy-start
  248.5 2.1 copy-start.3
  248.5 2.1 copy-start.4
  250.7 2.0 copy-start.1
  250.7 2.4 copy-start.2

commit v2 on v1

v2 whole, which is shorter than its diff:
```python
import functools

import jax
import jax.numpy as jnp
from jax import lax
from jax.experimental import pallas as pl
from jax.experimental.pallas import tpu as pltpu
from jax.sharding import PartitionSpec as P

BF = jnp.bfloat16
F32 = jnp.float32
MESH = pl.DeviceIdType.MESH
GX, GZ, GY = 4, 8, 2
CHUNKS = 4
PIECES_G, PIECES_D = 8, 4
CFG = dict(ahead=6, first=12, per=6, lag=6)
SLOTS = 8
LANES = 128
VMEM_BYTES = 60 * 2**20

ROWS_BY_ROWS = (((1,), (1,)), ((), ()))
COLS_BY_COLS = (((0,), (0,)), ((), ()))


def pick_tile(width, largest):
    tile = min(width, largest)
    while width % tile:
        tile -= LANES
    return tile


def offsets_of(i):
    place, code = i // (GX * GY), i % (GX * GY)
    odd = place % 2
    dz = odd * ((place + 1) // 2) + (1 - odd) * ((GZ - place // 2) % GZ)
    return code // GY, dz, code % GY


def shifted(me, dx, dz, dy):
    x, z, y = me // (GZ * GY), (me // GY) % GZ, me % GY
    return ((x + dx) % GX) * (GZ * GY) + ((z + dz) % GZ) * GY + (y + dy) % GY


def partner(me, i, sign):
    dx, dz, dy = offsets_of(i)
    if sign < 0:
        dx, dz = GX - dx, GZ - dz
    return shifted(me, dx, dz, dy)


def replica(dp, i):
    crosses = (i % GY) * (dp % 2)
    return dp + crosses * (2 - 4 * (dp // 2))


def codes_of(me, first, rows, dim, flag_ref):
    experts = flag_ref.shape[1]
    if dim == 0:
        row = first + lax.broadcasted_iota(jnp.int32, (rows, experts), 0)
        slot = shifted(me, row // (SLOTS * GY), 0, (row // SLOTS) % GY)
        lane = lax.broadcasted_iota(jnp.int32, (rows, experts), 1)
        hit = jnp.where(lane == slot, 1.0, 0.0) * flag_ref[...].astype(F32)
        moved = jnp.max(hit, axis=1, keepdims=True)
        row, slot = row[:, :1], slot[:, :1]
    else:
        row = first + lax.broadcasted_iota(jnp.int32, (experts, rows), 1)
        slot = partner(me, row // SLOTS, 1)
        line = lax.broadcasted_iota(jnp.int32, (experts, rows), 0)
        hit = jnp.where(line == slot, 1.0, 0.0).astype(BF)
        flags = jnp.broadcast_to(flag_ref[...].astype(F32), (16, experts)).astype(BF)
        moved = jnp.dot(flags, hit, preferred_element_type=F32)[:1, :]
        row, slot = row[:1, :], slot[:1, :]
    home = jnp.where(moved > 0.5, slot ^ (experts // 2), slot)
    return home * SLOTS + row % SLOTS


def exchange_kernel(
    parts, sizes, route_ref, slot_ref, weight_ref, flag_ref, tok_ref, cot_ref, wg_ref, wd_ref,
    ret_ref, own_g, own_d, far_g, far_d,
    sendb, recvb, mig_g, mig_d, full_g, full_d, rows_b, scaled_b, hid_b, both_b,
    retb, part_g, sib_g, sib_d, gathered, meta,
    ring_send, ring_recv, meta_send, meta_recv, a2a_send, a2a_recv, ret_send, ret_recv,
    mig_send, mig_recv, far_send, far_recv, sib_send, sib_recv, fwd_send, fwd_recv,
    red_send, red_recv, out_send, out_recv,
):
    experts, width, ff = sizes
    block = experts // CHUNKS
    chunk = block * SLOTS
    half = width // 2
    quarter_g, quarter_d = width // 4, ff // 4
    tokens = tok_ref.shape[0]
    dp = lax.axis_index("dp")
    me = lax.axis_index("expert")
    sib, far = dp ^ 1, dp ^ 2

    def remote(src, dst, send, recv, where):
        return pltpu.make_async_remote_copy(
            src_ref=src, dst_ref=dst, send_sem=send, recv_sem=recv,
            device_id=where, device_id_type=MESH,
        )

    step_g, step_d = quarter_g // PIECES_G, quarter_d // PIECES_D
    pieces = [(True, k * step_g, step_g) for k in range(PIECES_G)]
    pieces += [(False, k * step_d, step_d) for k in range(PIECES_D)]
    if "W" not in parts:
        pieces = []
    swaps, fars, sibs, fwds = [], [], [], []

    def swap(k):
        if k >= len(pieces):
            return
        is_g, off, count = pieces[k]
        src, dst = (wg_ref, mig_g) if is_g else (wd_ref, mig_d)
        rows = pl.ds(off, count)
        copy = remote(
            src.at[rows], dst.at[rows], mig_send.at[k], mig_recv.at[k], (dp, me ^ (experts // 2))
        )
        copy.start()
        swaps.append(copy)

    def gather(k):
        is_g, off, count = pieces[k]
        if is_g:
            own, mig, full, quarter = wg_ref, mig_g, full_g, quarter_g
        else:
            own, mig, full, quarter = wd_ref, mig_d, full_d, quarter_d
        swaps[k].wait_recv()
        rows = pl.ds(off, count)
        place = pl.ds(pl.multiple_of(dp * quarter + off, 16), count)
        full[place, :] = jnp.where(flagged, mig[rows, :], own[rows, :])
        copy = remote(full.at[place], full.at[place], far_send.at[k], far_recv.at[k], (far, me))
        copy.start()
        fars.append(copy)
        copy = remote(full.at[place], full.at[place], sib_send.at[k], sib_recv.at[k], (sib, me))
        copy.start()
        sibs.append(copy)

    def forward(k):
        is_g, off, count = pieces[k]
        full, quarter = (full_g, quarter_g) if is_g else (full_d, quarter_d)
        fars[k].wait_recv()
        place = pl.ds(pl.multiple_of(far * quarter + off, 16), count)
        copy = remote(full.at[place], full.at[place], fwd_send.at[k], fwd_recv.at[k], (sib, me))
        copy.start()
        fwds.append(copy)

    prep_tile = pick_tile(width, 512)
    plane = GX * GY
    picked = plane * SLOTS

    def rows_at(dz, part):
        return pl.ds((2 * (dz - 1) + part) * tokens, tokens)

    def block_at(dz, part):
        return gathered.at[rows_at(dz, part)]

    def hop(src, dz, part, way):
        where = (dp, shifted(me, 0, way % GZ, 0))
        k = 2 * (dz - 1) + part
        copy = remote(src, block_at(dz, part), ring_send.at[k], ring_recv.at[k], where)
        copy.start()
        hops.append(copy)

    def landed(dz, part):
        k = 2 * (dz - 1) + part
        here = block_at(dz, part)
        pltpu.make_async_copy(here, here, ring_recv.at[k]).wait()
        if dz < GZ // 2 - 1 or (dz == GZ // 2 - 1 and part == 0):
            hop(here, dz + 1, part, 1)
        if dz > GZ // 2 + 1 or (dz == GZ // 2 + 1 and part == 1):
            hop(here, dz - 1, part, -1)

    def dispatch(place):
        dz = offsets_of(place * plane)[1]
        pick = jnp.zeros((picked, tokens), F32)
        pick_w = jnp.zeros((picked, tokens), F32)
        for k in range(3):
            hit = codes == meta[dz, k : k + 1, :]
            pick = jnp.where(hit, 1.0, pick)
            pick_w = jnp.where(hit, meta[dz, 4 + k : 5 + k, :], pick_w)
        pick = pick.astype(BF)
        pick_w = pick_w.astype(BF)
        first = place * plane
        for col in range(0, width, prep_tile):
            cols = slice(col, col + prep_tile)
            tok = tok_ref[:, cols] if dz == 0 else gathered[rows_at(dz, 0), cols]
            cot = cot_ref[:, cols] if dz == 0 else gathered[rows_at(dz, 1), cols]
            rows = jnp.dot(pick, tok, preferred_element_type=F32)
            cots = jnp.dot(pick_w, cot, preferred_element_type=F32)
            both = jnp.concatenate(
                [rows.reshape(plane, SLOTS, prep_tile), cots.reshape(plane, SLOTS, prep_tile)],
                axis=1,
            )
            sendb[first : first + plane, :, cols] = both.astype(BF)
        chunk_sem = a2a_recv.at[first // block]
        pltpu.make_async_copy(sendb.at[first], recvb.at[first], chunk_sem).start()

        def send(j, carry):
            where = (replica(dp, j), shifted(me, j // GY, 0, j % GY))
            i = first + j
            remote(sendb.at[i], recvb.at[i], a2a_send, chunk_sem, where).start()
            return carry

        lax.fori_loop(1, plane, send, 0)

    ahead, lag = CFG['ahead'], CFG['lag']
    for k in range(ahead):
        swap(k)
    hops = []
    if "D" in parts:
        meta[0] = jnp.zeros((SLOTS, tokens), F32)
        for k in range(3):
            code = route_ref[k : k + 1, :] * SLOTS + slot_ref[k : k + 1, :]
            meta[0, k : k + 1, :] = code.astype(F32)
            meta[0, 4 + k : 5 + k, :] = weight_ref[k : k + 1, :].astype(BF).astype(F32)
        for part, src in ((0, tok_ref), (1, cot_ref)):
            hop(src, 1, part, 1)
            hop(src, GZ - 1, part, -1)

        def send_meta(dz, carry):
            where = (dp, shifted(me, 0, dz, 0))
            remote(meta.at[0], meta.at[dz], meta_send, meta_recv, where).start()
            return carry

        lax.fori_loop(1, GZ, send_meta, 0)
        codes = codes_of(me, 0, picked, 0, flag_ref).astype(F32)
    lane = lax.broadcasted_iota(jnp.int32, flag_ref.shape, 1)
    mine = jnp.where(lane == me, flag_ref[...], 0).astype(F32)
    flagged = jnp.max(mine, axis=1, keepdims=True) > 0.5

    done = 0

    def weights(count):
        nonlocal done
        for k in range(done, min(done + count, len(pieces) + lag)):
            if k < len(pieces):
                gather(k)
                swap(k + ahead)
            if k >= lag:
                forward(k - lag)
            done = k + 1

    if "D" in parts:
        dispatch(0)
        others = meta.at[pl.ds(1, GZ - 1)]
        pltpu.make_async_copy(others, others, meta_recv).wait()
        for t in range(1, GZ // 2):
            for part in range(2):
                landed(t, part)
                landed(GZ - t, part)
            dispatch(2 * t - 1)
            dispatch(2 * t)
            weights(CFG["per"])
        for part in range(2):
            landed(GZ // 2, part)
        dispatch(GZ - 1)
    weights(len(pieces) + lag)
    for k in range(len(pieces)):
        sibs[k].wait_recv()
        fwds[k].wait_recv()

    ff_tile = pick_tile(ff, 256)
    half_tile = pick_tile(half, 256)

    def expert(c):
        first = c * block
        place = pl.ds(c * chunk, chunk)
        for col in range(0, width, prep_tile):
            cols = slice(col, col + prep_tile)
            both = recvb[pl.ds(first, block), :, cols].astype(F32)
            rows_b[place, cols] = both[:, :SLOTS].reshape(chunk, prep_tile).astype(BF)
            scaled_b[place, cols] = both[:, SLOTS:].reshape(chunk, prep_tile).astype(BF)
        prob = jnp.zeros((chunk, 1), F32)
        for f in range(0, ff, ff_tile):
            cols = slice(f, f + ff_tile)
            up_cols = slice(ff + f, ff + f + ff_tile)
            rows = rows_b[place, :]
            gate = jnp.dot(rows, full_g[:, cols], preferred_element_type=F32)
            up = jnp.dot(rows, full_g[:, up_cols], preferred_element_type=F32)
            hgrad = lax.dot_general(
                scaled_b[place, :], full_d[cols, :], ROWS_BY_ROWS, preferred_element_type=F32
            )
            sig = jax.nn.sigmoid(gate)
            silu = gate * sig
            hid = (silu * up).astype(BF)
            hid_b[place, cols] = hid
            both_b[place, cols] = (hgrad * up * sig * (1.0 + gate * (1.0 - sig))).astype(BF)
            both_b[place, up_cols] = (hgrad * silu).astype(BF)
            prob = prob + jnp.sum(hid.astype(F32) * hgrad, axis=1, keepdims=True)
        prob = jnp.broadcast_to(prob, (chunk, LANES))
        rough = prob.astype(BF).astype(F32)
        both = jnp.concatenate(
            [rough.reshape(block, SLOTS, LANES), (prob - rough).reshape(block, SLOTS, LANES)],
            axis=1,
        )
        retb[pl.ds(first, block), :, half : half + LANES] = both.astype(BF)

    def row_grads(c):
        first = c * block
        place = pl.ds(c * chunk, chunk)
        for col in range(0, half, half_tile):
            lo = lax.dot_general(
                both_b[place, :], full_g[col : col + half_tile, :], ROWS_BY_ROWS,
                preferred_element_type=F32,
            )
            hi = lax.dot_general(
                both_b[place, :], full_g[half + col : half + col + half_tile, :], ROWS_BY_ROWS,
                preferred_element_type=F32,
            )
            both = jnp.concatenate(
                [lo.reshape(block, SLOTS, half_tile), hi.reshape(block, SLOTS, half_tile)], axis=1
            )
            retb[pl.ds(first, block), :, col : col + half_tile] = both.astype(BF)

    def give_back(c):
        if "R" not in parts:
            return

        def send(j, carry):
            i = c * block + j

            @pl.when(i > 0)
            def _():
                remote(
                    retb.at[i], ret_ref.at[i], ret_send, ret_recv,
                    (replica(dp, i), partner(me, i, -1)),
                ).start()

            return carry

        lax.fori_loop(0, block, send, 0)

    def arrive(c):
        if "D" in parts:
            arrived = recvb.at[pl.ds(c * block, block)]
            pltpu.make_async_copy(arrived, arrived, a2a_recv.at[c]).wait()

    def early(c, carry):
        first = recvb.at[pl.ds(c * block, block)]
        if "D" in parts:
            pltpu.make_async_copy(first, first, a2a_recv.at[c]).wait()
        if "C" in parts:
            expert(c)
            row_grads(c)
        give_back(c)
        return carry

    lax.fori_loop(0, CHUNKS - 1, early, 0)
    if "R" in parts:
        pltpu.make_async_copy(retb.at[0], ret_ref.at[0], ret_recv).start()
    last = CHUNKS - 1
    arrive(last)
    if "C" in parts:
        expert(last)

    wide = pick_tile(2 * ff, 768)
    d_tile = pick_tile(quarter_g, 256)

    def gate_up_grads(quarter):
        if "G" not in parts:
            return

        def tile(i, carry):
            start = pl.multiple_of(quarter * quarter_g + i * d_tile, d_tile)
            left = rows_b[:, pl.ds(start, d_tile)]
            for c in range(0, 2 * ff, wide):
                part_g[pl.ds(start, d_tile), c : c + wide] = lax.dot_general(
                    left, both_b[:, c : c + wide], COLS_BY_COLS, preferred_element_type=F32
                ).astype(BF)
            return carry

        lax.fori_loop(0, quarter_g // d_tile, tile, 0)

    part_d = gathered

    def down_grads():
        for copy in hops:
            copy.wait_send()
        if "G" not in parts:
            return
        for f in range(0, ff, ff_tile):
            for c in range(0, width, prep_tile):
                part_d[f : f + ff_tile, c : c + prep_tile] = lax.dot_general(
                    hid_b[:, f : f + ff_tile], scaled_b[:, c : c + prep_tile], COLS_BY_COLS,
                    preferred_element_type=F32,
                ).astype(BF)

    def place_of(quarter, rows):
        return pl.ds(pl.multiple_of(quarter * rows, 16), rows)

    reds = []

    def to_sibling(slot, part, rows, landing, quarter, where):
        if "S" not in parts:
            return
        copy = remote(
            part.at[place_of(quarter, rows)], landing.at[where],
            red_send.at[slot], red_recv.at[slot], (sib, me),
        )
        copy.start()
        reds.append(copy)

    outs = []

    def to_far(slot, part, rows, landing, out):
        if "S" not in parts:
            return
        reds[slot].wait_recv()
        total = part[place_of(far, rows), :].astype(F32) + landing[0].astype(F32)
        landing[0] = total.astype(BF)
        copy = remote(landing.at[0], out, out_send.at[slot], out_recv.at[slot], (far, me))
        copy.start()
        outs.append(copy)

    gate_up_grads(far ^ 1)
    to_sibling(0, part_g, quarter_g, sib_g, far ^ 1, 0)
    gate_up_grads(far)
    to_far(0, part_g, quarter_g, sib_g, far_g)
    if "C" in parts:
        row_grads(last)
    give_back(last)
    down_grads()
    to_sibling(1, part_d, quarter_d, sib_d, far ^ 1, 0)
    to_sibling(2, part_d, quarter_d, sib_d, dp ^ 1, 1)
    gate_up_grads(dp ^ 1)
    to_sibling(3, part_g, quarter_g, sib_g, dp ^ 1, 1)
    to_far(1, part_d, quarter_d, sib_d, far_d)
    gate_up_grads(dp)
    if "S" in parts:
        reds[2].wait_recv()
        own_d[...] = (
            part_d[place_of(dp, quarter_d), :].astype(F32) + sib_d[1].astype(F32)
        ).astype(BF)
        reds[3].wait_recv()
        own_g[...] = (
            part_g[place_of(dp, quarter_g), :].astype(F32) + sib_g[1].astype(F32)
        ).astype(BF)

    if "D" in parts:
        others = sendb.at[pl.ds(0, experts - GZ)]
        pltpu.make_async_copy(others, others, a2a_send).wait()
        others = meta.at[pl.ds(1, GZ - 1)]
        pltpu.make_async_copy(others, others, meta_send).wait()
    for copy in swaps + fars + sibs + fwds + reds:
        copy.wait_send()
    if "R" in parts:
        others = retb.at[pl.ds(1, experts - 1)]
        pltpu.make_async_copy(others, others, ret_send).wait()
        pltpu.make_async_copy(retb, retb, ret_recv).wait()
    for copy in outs:
        copy.wait()


def combine_kernel(ret_ref, route_ref, slot_ref, weight_ref, flag_ref, tok_out, weight_out):
    experts, _, cols = ret_ref.shape
    half = cols - LANES
    rows = experts * SLOTS
    codes = codes_of(lax.axis_index("expert"), 0, rows, 1, flag_ref)
    tokens = route_ref.shape[1]
    hits = []
    for k in range(3):
        code = (route_ref[k : k + 1, :] * SLOTS + slot_ref[k : k + 1, :]).astype(F32)
        hits.append(codes == jnp.broadcast_to(code, (LANES, tokens)).T[:, :1].astype(jnp.int32))
    pick = jnp.zeros(hits[0].shape, F32)
    for hit in hits:
        pick = jnp.where(hit, 1.0, pick)
    pick = pick.astype(BF)
    tile = pick_tile(half, 512)
    for c in range(0, half, tile):
        both = ret_ref[:, :, c : c + tile].astype(F32)
        lo = both[:, :SLOTS].reshape(rows, tile).astype(BF)
        hi = both[:, SLOTS:].reshape(rows, tile).astype(BF)
        tok_out[:, c : c + tile] = jnp.dot(pick, lo, preferred_element_type=F32)
        tok_out[:, half + c : half + c + tile] = jnp.dot(pick, hi, preferred_element_type=F32)
    both = ret_ref[:, :, half:].astype(F32)
    rough = both[:, :SLOTS].reshape(rows, LANES).astype(BF)
    rest = both[:, SLOTS:].reshape(rows, LANES).astype(BF)
    for k in range(3):
        one = jnp.where(hits[k], 1.0, 0.0).astype(BF)
        prob = jnp.dot(one, rough, preferred_element_type=F32)
        prob = prob + jnp.dot(one, rest, preferred_element_type=F32)
        weight_out[k : k + 1, :] = prob.T[:1, :] / weight_ref[k : k + 1, :].astype(BF).astype(F32)


def body(parts, tokens, cotangent, routes, slot_index, route_weight, swap_flags, w_gate_up, w_down):
    tok_rows, width = tokens.shape
    experts = swap_flags.shape[0]
    ff = w_down.shape[1] * lax.axis_size("dp")
    rows = experts * SLOTS
    quarter_g, quarter_d = w_gate_up.shape[1], w_down.shape[1]
    pieces = PIECES_G + PIECES_D

    vmem = pl.BlockSpec(memory_space=pltpu.VMEM)
    hbm = pl.BlockSpec(memory_space=pl.ANY)
    dma = pltpu.SemaphoreType.DMA
    flops = 2 * rows * width * ff * 9
    ret, own_g, own_d, far_g, far_d = pl.pallas_call(
        functools.partial(exchange_kernel, parts, (experts, width, ff)),
        name="ex_" + "".join(parts),
        out_shape=(
            jax.ShapeDtypeStruct((experts, 2 * SLOTS, width // 2 + LANES), BF),
            jax.ShapeDtypeStruct((quarter_g, 2 * ff), BF),
            jax.ShapeDtypeStruct((quarter_d, width), BF),
            jax.ShapeDtypeStruct((quarter_g, 2 * ff), BF),
            jax.ShapeDtypeStruct((quarter_d, width), BF),
        ),
        in_specs=[vmem] * 8,
        out_specs=(hbm, vmem, vmem, hbm, hbm),
        scratch_shapes=[
            pltpu.VMEM((experts, 2 * SLOTS, width), BF),
            pltpu.VMEM((experts, 2 * SLOTS, width), BF),
            pltpu.VMEM((quarter_g, 2 * ff), BF),
            pltpu.VMEM((quarter_d, width), BF),
            pltpu.VMEM((width, 2 * ff), BF),
            pltpu.VMEM((ff, width), BF),
            pltpu.VMEM((rows, width), BF),
            pltpu.VMEM((rows, width), BF),
            pltpu.VMEM((rows, ff), BF),
            pltpu.VMEM((rows, 2 * ff), BF),
            pltpu.VMEM((experts, 2 * SLOTS, width // 2 + LANES), BF),
            pltpu.VMEM((width, 2 * ff), BF),
            pltpu.VMEM((2, quarter_g, 2 * ff), BF),
            pltpu.VMEM((2, quarter_d, width), BF),
            pltpu.VMEM((2 * (GZ - 1) * tok_rows, width), BF),
            pltpu.VMEM((GZ, SLOTS, tok_rows), F32),
            dma((2 * GZ - 2,)), dma((2 * GZ - 2,)), dma, dma,
            dma, dma((CHUNKS,)), dma, dma,
            dma((pieces,)), dma((pieces,)), dma((pieces,)), dma((pieces,)),
            dma((pieces,)), dma((pieces,)), dma((pieces,)), dma((pieces,)),
            dma((4,)), dma((4,)), dma((2,)), dma((2,)),
        ],
        compiler_params=pltpu.CompilerParams(
            has_side_effects=True, vmem_limit_bytes=VMEM_BYTES
        ),
        cost_estimate=pl.CostEstimate(
            flops=flops, bytes_accessed=12 * 2**20, transcendentals=rows * ff
        ),
    )(
        routes.T, slot_index.T, route_weight.T, swap_flags[None], tokens, cotangent, w_gate_up[0], w_down[0]
    )

    grad_tokens, grad_weight = pl.pallas_call(
        combine_kernel,
        name="combine",
        out_shape=(
            jax.ShapeDtypeStruct((tok_rows, width), F32),
            jax.ShapeDtypeStruct((3, tok_rows), F32),
        ),
        in_specs=[vmem] * 5,
        out_specs=(vmem, vmem),
        compiler_params=pltpu.CompilerParams(vmem_limit_bytes=32 * 2**20),
    )(ret, routes.T, slot_index.T, route_weight.T, swap_flags[None])
    grad_gu = (own_g.astype(F32) + far_g.astype(F32))[None]
    grad_dn = (own_d.astype(F32) + far_d.astype(F32))[None]
    return (grad_tokens, grad_weight.T, grad_gu, grad_dn)


def solution(mesh):
    return jax.shard_map(
        functools.partial(body, 'DWCGRS'),
        mesh=mesh,
        in_specs=(
            P(("dp", "expert"), None),
            P(("dp", "expert"), None),
            P(("dp", "expert"), None),
            P(("dp", "expert"), None),
            P(("dp", "expert"), None),
            P(),
            P("expert", "dp", None),
            P("expert", "dp", None),
        ),
        out_specs=(
            P(("dp", "expert"), None),
            P(("dp", "expert"), None),
            P("expert", "dp", None),
            P("expert", "dp", None),
        ),
        check_vma=False,
    )
```

time: 256 us -> 216 us (0.84)
  Pallas kernels: 244 us -> 206 us
  other arithmetic: 6.27 us -> 3.48 us
    pallas_call x1, Pallas kernels: 242 us -> 205 us  [body(): pl.pallas_call(functools.partial(exchange_kernel, parts, (experts, width,...]
where the time goes in v2:
time: 216 us; the launch traced here: 213 us
  Pallas kernels  206 us (95%)
  other arithmetic  3.48 us (2%)
  local copies, waits for them, and re-layouts  2.75 us (1%)
    pallas_call x1, Pallas kernels, body(): pl.pallas_call(functools.partial(exchange_kernel, parts, (experts, width,...  205 us

profile of v2, /device:TPU:1, one launch (start us, length us, event | category | flops | bytes accessed | tf_op | source)
XLA Modules:
  0.0 213.3 jit_solution(9468195646896067353)
XLA Ops:
  0.6 0.0 copy-start.1
  0.6 0.0 copy-start.2
  0.7 0.0 copy-start.3
  0.7 0.0 copy-start.4
  0.7 204.7 %ex_DWCGRS.1 = (bf16[64,16,1152]{2,1,0:T(8,128)(2,1)}, bf16[512,1536]{1,0:T(8,128)(2,1)}, bf16[192,2048]{1,0:T(8,128)(2,1)}, bf16[512,1536]{1,0:T(8,128)(2,1)}, bf16[192,2048]{1,0:T(8,128)(2,1)}) custom-call(s32[3,128]{1,0:T(4,128)} %bitcast.11, s32[3,128]{1,0:T(4,128)} %bitcast.13, f32[3,128]{1,0:T(4,128)} %bitcast.15, s32[1,64]{1,0:T(1,128)} %bitcast.17, ...), custom_call_target="tpu_custom_call" | custom-call | flops 14495514624 | bytes 12582912 | tf_op jit(solution)/shard_map/ex_DWCGRS/pallas_call | solution.py:497
  205.4 0.0 copy-done.1
  205.4 0.0 copy-done.2
  205.4 0.0 copy-done.3
  205.4 0.0 copy-done.4
  205.5 0.0 copy-start
  205.5 1.7 copy-done
  207.1 0.0 copy-start.7
  207.1 0.0 copy-start.8
  207.1 1.6 combine.1
  208.8 0.0 copy-done.7
  208.8 0.0 copy-done.8
  208.8 0.0 copy-start.5
  208.8 0.0 copy-start.6
  208.8 1.4 add_bitcast_fusion.1
  210.1 0.6 copy-done.5
  210.7 0.5 copy-done.6
  211.2 2.1 add_bitcast_fusion
Async XLA Ops:
  0.6 204.8 %copy-start.1 = (s32[128,3]{0,1:T(4,128)S(1)}, s32[128,3]{0,1:T(4,128)}, u32[]{:S(2)}) copy-start(s32[128,3]{0,1:T(4,128)} %param.10) | copy-start | bytes 4612
  0.6 204.8 %copy-start.2 = (s32[128,3]{0,1:T(4,128)S(1)}, s32[128,3]{0,1:T(4,128)}, u32[]{:S(2)}) copy-start(s32[128,3]{0,1:T(4,128)} %param.11) | copy-start | bytes 4612
  0.7 204.8 %copy-start.3 = (f32[128,3]{0,1:T(4,128)S(1)}, f32[128,3]{0,1:T(4,128)}, u32[]{:S(2)}) copy-start(f32[128,3]{0,1:T(4,128)} %param.12) | copy-start | bytes 4612
  0.7 204.8 %copy-start.4 = (s32[64]{0:T(128)S(1)}, s32[64]{0:T(128)}, u32[]{:S(2)}) copy-start(s32[64]{0:T(128)} %param.13) | copy-start | bytes 772
  205.5 1.7 copy-start
  207.1 1.6 copy-start.7
  207.1 1.6 copy-start.8
  208.8 2.0 copy-start.5
  208.8 2.4 %copy-start.6 = (bf16[512,1536]{1,0:T(8,128)(2,1)S(1)}, bf16[512,1536]{1,0:T(8,128)(2,1)}, u32[]{:S(2)}) copy-start(bf16[512,1536]{1,0:T(8,128)(2,1)} %get-tuple-element.15) | copy-start | bytes 4718596

commit v3 on v2

--- a/solution.py
+++ b/solution.py
@@ -13,10 +13,11 @@
 GX, GZ, GY = 4, 8, 2
 CHUNKS = 4
 PIECES_G, PIECES_D = 8, 4
-CFG = dict(ahead=6, first=12, per=6, lag=6)
+AHEAD, FIRST = 12, 6
+DEFER = 0
 SLOTS = 8
 LANES = 128
-VMEM_BYTES = 60 * 2**20
+VMEM_BYTES = 61 * 2**20
 
 ROWS_BY_ROWS = (((1,), (1,)), ((), ()))
 COLS_BY_COLS = (((0,), (0,)), ((), ()))
@@ -78,7 +79,7 @@
     parts, sizes, route_ref, slot_ref, weight_ref, flag_ref, tok_ref, cot_ref, wg_ref, wd_ref,
     ret_ref, own_g, own_d, far_g, far_d,
     sendb, recvb, mig_g, mig_d, full_g, full_d, rows_b, scaled_b, hid_b, both_b,
-    retb, part_g, sib_g, sib_d, gathered, meta,
+    retb, part_g, sib_g, sib_d, gathered, meta, gate_up,
     ring_send, ring_recv, meta_send, meta_recv, a2a_send, a2a_recv, ret_send, ret_recv,
     mig_send, mig_recv, far_send, far_recv, sib_send, sib_recv, fwd_send, fwd_recv,
     red_send, red_recv, out_send, out_recv,
@@ -170,7 +171,7 @@
         if dz > GZ // 2 + 1 or (dz == GZ // 2 + 1 and part == 1):
             hop(here, dz - 1, part, -1)
 
-    def dispatch(place):
+    def prepare(place):
         dz = offsets_of(place * plane)[1]
         pick = jnp.zeros((picked, tokens), F32)
         pick_w = jnp.zeros((picked, tokens), F32)
@@ -192,6 +193,9 @@
                 axis=1,
             )
             sendb[first : first + plane, :, cols] = both.astype(BF)
+
+    def push(place):
+        first = place * plane
         chunk_sem = a2a_recv.at[first // block]
         pltpu.make_async_copy(sendb.at[first], recvb.at[first], chunk_sem).start()
 
@@ -203,8 +207,7 @@
 
         lax.fori_loop(1, plane, send, 0)
 
-    ahead, lag = CFG['ahead'], CFG['lag']
-    for k in range(ahead):
+    for k in range(AHEAD):
         swap(k)
     hops = []
     if "D" in parts:
@@ -228,55 +231,31 @@
     mine = jnp.where(lane == me, flag_ref[...], 0).astype(F32)
     flagged = jnp.max(mine, axis=1, keepdims=True) > 0.5
 
-    done = 0
-
-    def weights(count):
-        nonlocal done
-        for k in range(done, min(done + count, len(pieces) + lag)):
-            if k < len(pieces):
-                gather(k)
-                swap(k + ahead)
-            if k >= lag:
-                forward(k - lag)
-            done = k + 1
-
-    if "D" in parts:
-        dispatch(0)
-        others = meta.at[pl.ds(1, GZ - 1)]
-        pltpu.make_async_copy(others, others, meta_recv).wait()
-        for t in range(1, GZ // 2):
-            for part in range(2):
-                landed(t, part)
-                landed(GZ - t, part)
-            dispatch(2 * t - 1)
-            dispatch(2 * t)
-            weights(CFG["per"])
-        for part in range(2):
-            landed(GZ // 2, part)
-        dispatch(GZ - 1)
-    weights(len(pieces) + lag)
-    for k in range(len(pieces)):
-        sibs[k].wait_recv()
-        fwds[k].wait_recv()
-
     ff_tile = pick_tile(ff, 256)
     half_tile = pick_tile(half, 256)
 
-    def expert(c):
-        first = c * block
-        place = pl.ds(c * chunk, chunk)
+    def forward_part(first, count):
+        rows_n = count * SLOTS
+        place = pl.ds(first * SLOTS, rows_n)
         for col in range(0, width, prep_tile):
             cols = slice(col, col + prep_tile)
-            both = recvb[pl.ds(first, block), :, cols].astype(F32)
-            rows_b[place, cols] = both[:, :SLOTS].reshape(chunk, prep_tile).astype(BF)
-            scaled_b[place, cols] = both[:, SLOTS:].reshape(chunk, prep_tile).astype(BF)
-        prob = jnp.zeros((chunk, 1), F32)
+            both = recvb[first : first + count, :, cols].astype(F32)
+            rows_b[place, cols] = both[:, :SLOTS].reshape(rows_n, prep_tile).astype(BF)
+            scaled_b[place, cols] = both[:, SLOTS:].reshape(rows_n, prep_tile).astype(BF)
+        for f in range(0, 2 * ff, ff_tile):
+            cols = slice(f, f + ff_tile)
+            gate_up[:rows_n, cols] = jnp.dot(
+                rows_b[place, :], full_g[:, cols], preferred_element_type=F32
+            )
+
+    def backward_part(first, count):
+        rows_n = count * SLOTS
+        place = pl.ds(first * SLOTS, rows_n)
+        prob = jnp.zeros((rows_n, 1), F32)
         for f in range(0, ff, ff_tile):
             cols = slice(f, f + ff_tile)
             up_cols = slice(ff + f, ff + f + ff_tile)
-            rows = rows_b[place, :]
-            gate = jnp.dot(rows, full_g[:, cols], preferred_element_type=F32)
-            up = jnp.dot(rows, full_g[:, up_cols], preferred_element_type=F32)
+            gate, up = gate_up[:rows_n, cols], gate_up[:rows_n, up_cols]
             hgrad = lax.dot_general(
                 scaled_b[place, :], full_d[cols, :], ROWS_BY_ROWS, preferred_element_type=F32
             )
@@ -287,17 +266,16 @@
             both_b[place, cols] = (hgrad * up * sig * (1.0 + gate * (1.0 - sig))).astype(BF)
             both_b[place, up_cols] = (hgrad * silu).astype(BF)
             prob = prob + jnp.sum(hid.astype(F32) * hgrad, axis=1, keepdims=True)
-        prob = jnp.broadcast_to(prob, (chunk, LANES))
+        prob = jnp.broadcast_to(prob, (rows_n, LANES))
         rough = prob.astype(BF).astype(F32)
         both = jnp.concatenate(
-            [rough.reshape(block, SLOTS, LANES), (prob - rough).reshape(block, SLOTS, LANES)],
+            [rough.reshape(count, SLOTS, LANES), (prob - rough).reshape(count, SLOTS, LANES)],
             axis=1,
         )
-        retb[pl.ds(first, block), :, half : half + LANES] = both.astype(BF)
-
-    def row_grads(c):
-        first = c * block
-        place = pl.ds(c * chunk, chunk)
+        retb[first : first + count, :, half : half + LANES] = both.astype(BF)
+
+    def row_grads(first, count):
+        place = pl.ds(first * SLOTS, count * SLOTS)
         for col in range(0, half, half_tile):
             lo = lax.dot_general(
                 both_b[place, :], full_g[col : col + half_tile, :], ROWS_BY_ROWS,
@@ -308,9 +286,9 @@
                 preferred_element_type=F32,
             )
             both = jnp.concatenate(
-                [lo.reshape(block, SLOTS, half_tile), hi.reshape(block, SLOTS, half_tile)], axis=1
+                [lo.reshape(count, SLOTS, half_tile), hi.reshape(count, SLOTS, half_tile)], axis=1
             )
-            retb[pl.ds(first, block), :, col : col + half_tile] = both.astype(BF)
+            retb[first : first + count, :, col : col + half_tile] = both.astype(BF)
 
     def give_back(c):
         if "R" not in parts:
@@ -335,23 +313,74 @@
             arrived = recvb.at[pl.ds(c * block, block)]
             pltpu.make_async_copy(arrived, arrived, a2a_recv.at[c]).wait()
 
-    def early(c, carry):
-        first = recvb.at[pl.ds(c * block, block)]
+    def weights(gathers, forwards):
+        for k in gathers:
+            if k < len(pieces):
+                gather(k)
+                swap(k + AHEAD)
+        for k in forwards:
+            if k < len(pieces):
+                forward(k)
+
+    total = PIECES_G + PIECES_D
+    plan = {
+        1: (range(FIRST), ()),
+        2: (range(FIRST, total), range(FIRST)),
+        3: ((), range(FIRST, total)),
+    }
+    if "D" in parts:
+        prepare(0)
+        if DEFER == 0:
+            push(0)
+        others = meta.at[pl.ds(1, GZ - 1)]
+        pltpu.make_async_copy(others, others, meta_recv).wait()
+    for t in range(1, GZ // 2):
         if "D" in parts:
-            pltpu.make_async_copy(first, first, a2a_recv.at[c]).wait()
-        if "C" in parts:
-            expert(c)
-            row_grads(c)
-        give_back(c)
-        return carry
-
-    lax.fori_loop(0, CHUNKS - 1, early, 0)
+            for part in range(2):
+                landed(t, part)
+                landed(GZ - t, part)
+        if t <= DEFER:
+            weights(*plan[t])
+        if "D" in parts:
+            for place in (2 * t - 1, 2 * t):
+                prepare(place)
+                if t > DEFER:
+                    push(place)
+            if t == DEFER:
+                for place in range(2 * t + 1):
+                    push(place)
+        if t > DEFER:
+            weights(*plan[t])
+    if "D" in parts:
+        for part in range(2):
+            landed(GZ // 2, part)
+        prepare(GZ - 1)
+        push(GZ - 1)
+
+    def complete(first, stop):
+        for k in range(first, min(stop, len(pieces))):
+            sibs[k].wait_recv()
+            fwds[k].wait_recv()
+
+    last = CHUNKS - 1
+    ahead = last * block
+    for c in range(last):
+        arrive(c)
+    complete(0, PIECES_G)
+    if "C" in parts:
+        forward_part(0, ahead)
+    complete(PIECES_G, total)
+    if "C" in parts:
+        backward_part(0, ahead)
+        row_grads(0, ahead)
     if "R" in parts:
         pltpu.make_async_copy(retb.at[0], ret_ref.at[0], ret_recv).start()
-    last = CHUNKS - 1
+    for c in range(last):
+        give_back(c)
     arrive(last)
     if "C" in parts:
-        expert(last)
+        forward_part(ahead, block)
+        backward_part(ahead, block)
 
     wide = pick_tile(2 * ff, 768)
     d_tile = pick_tile(quarter_g, 256)
@@ -417,7 +446,7 @@
     gate_up_grads(far)
     to_far(0, part_g, quarter_g, sib_g, far_g)
     if "C" in parts:
-        row_grads(last)
+        row_grads(ahead, block)
     give_back(last)
     down_grads()
     to_sibling(1, part_d, quarter_d, sib_d, far ^ 1, 0)
@@ -451,10 +480,27 @@
         copy.wait()
 
 
-def combine_kernel(ret_ref, route_ref, slot_ref, weight_ref, flag_ref, tok_out, weight_out):
+def finish_kernel(
+    ret_hbm, own_g, own_d, far_g, far_d, route_ref, slot_ref, weight_ref, flag_ref,
+    tok_out, weight_out, out_g, out_d,
+    ret_ref, a_g, b_g, a_d, b_d, sum_g, sum_d, tok_ref, in_sem, out_sem,
+):
     experts, _, cols = ret_ref.shape
     half = cols - LANES
     rows = experts * SLOTS
+    load_ret = pltpu.make_async_copy(ret_hbm, ret_ref, in_sem.at[0])
+    load_ret.start()
+    steps = 4
+    step_g, step_d = a_g.shape[0] // steps, a_d.shape[0] // steps
+    loads = []
+    for k in range(steps):
+        for n, (src, dst, step) in enumerate(
+            ((own_g, a_g, step_g), (far_g, b_g, step_g), (own_d, a_d, step_d), (far_d, b_d, step_d))
+        ):
+            part = pl.ds(k * step, step)
+            copy = pltpu.make_async_copy(src.at[part], dst.at[part], in_sem.at[1 + 4 * k + n])
+            copy.start()
+            loads.append(copy)
     codes = codes_of(lax.axis_index("expert"), 0, rows, 1, flag_ref)
     tokens = route_ref.shape[1]
     hits = []
@@ -465,13 +511,31 @@
     for hit in hits:
         pick = jnp.where(hit, 1.0, pick)
     pick = pick.astype(BF)
+    load_ret.wait()
+    stores = []
+
+    def store(src, dst, n):
+        copy = pltpu.make_async_copy(src, dst, out_sem.at[n])
+        copy.start()
+        stores.append(copy)
+
     tile = pick_tile(half, 512)
     for c in range(0, half, tile):
         both = ret_ref[:, :, c : c + tile].astype(F32)
         lo = both[:, :SLOTS].reshape(rows, tile).astype(BF)
         hi = both[:, SLOTS:].reshape(rows, tile).astype(BF)
-        tok_out[:, c : c + tile] = jnp.dot(pick, lo, preferred_element_type=F32)
-        tok_out[:, half + c : half + c + tile] = jnp.dot(pick, hi, preferred_element_type=F32)
+        tok_ref[:, c : c + tile] = jnp.dot(pick, lo, preferred_element_type=F32)
+        tok_ref[:, half + c : half + c + tile] = jnp.dot(pick, hi, preferred_element_type=F32)
+    store(tok_ref, tok_out, 0)
+    for k in range(steps):
+        for copy in loads[4 * k : 4 * k + 4]:
+            copy.wait()
+        part = pl.ds(k * step_g, step_g)
+        sum_g[part, :] = a_g[part, :].astype(F32) + b_g[part, :].astype(F32)
+        store(sum_g.at[part], out_g.at[part], 1 + 2 * k)
+        part = pl.ds(k * step_d, step_d)
+        sum_d[part, :] = a_d[part, :].astype(F32) + b_d[part, :].astype(F32)
+        store(sum_d.at[part], out_d.at[part], 2 + 2 * k)
     both = ret_ref[:, :, half:].astype(F32)
     rough = both[:, :SLOTS].reshape(rows, LANES).astype(BF)
     rest = both[:, SLOTS:].reshape(rows, LANES).astype(BF)
@@ -480,6 +544,8 @@
         prob = jnp.dot(one, rough, preferred_element_type=F32)
         prob = prob + jnp.dot(one, rest, preferred_element_type=F32)
         weight_out[k : k + 1, :] = prob.T[:1, :] / weight_ref[k : k + 1, :].astype(BF).astype(F32)
+    for copy in stores:
+        copy.wait()
 
 
 def body(parts, tokens, cotangent, routes, slot_index, route_weight, swap_flags, w_gate_up, w_down):
@@ -523,6 +589,7 @@
             pltpu.VMEM((2, quarter_d, width), BF),
             pltpu.VMEM((2 * (GZ - 1) * tok_rows, width), BF),
             pltpu.VMEM((GZ, SLOTS, tok_rows), F32),
+            pltpu.VMEM((rows // CHUNKS * (CHUNKS - 1), 2 * ff), F32),
             dma((2 * GZ - 2,)), dma((2 * GZ - 2,)), dma, dma,
             dma, dma((CHUNKS,)), dma, dma,
             dma((pieces,)), dma((pieces,)), dma((pieces,)), dma((pieces,)),
@@ -539,20 +606,35 @@
         routes.T, slot_index.T, route_weight.T, swap_flags[None], tokens, cotangent, w_gate_up[0], w_down[0]
     )
 
-    grad_tokens, grad_weight = pl.pallas_call(
-        combine_kernel,
-        name="combine",
+    grad_tokens, grad_weight, grad_gu, grad_dn = pl.pallas_call(
+        finish_kernel,
+        name="finish",
         out_shape=(
             jax.ShapeDtypeStruct((tok_rows, width), F32),
             jax.ShapeDtypeStruct((3, tok_rows), F32),
+            jax.ShapeDtypeStruct((quarter_g, 2 * ff), F32),
+            jax.ShapeDtypeStruct((quarter_d, width), F32),
         ),
-        in_specs=[vmem] * 5,
-        out_specs=(vmem, vmem),
-        compiler_params=pltpu.CompilerParams(vmem_limit_bytes=32 * 2**20),
-    )(ret, routes.T, slot_index.T, route_weight.T, swap_flags[None])
-    grad_gu = (own_g.astype(F32) + far_g.astype(F32))[None]
-    grad_dn = (own_d.astype(F32) + far_d.astype(F32))[None]
-    return (grad_tokens, grad_weight.T, grad_gu, grad_dn)
+        in_specs=[hbm] * 5 + [vmem] * 4,
+        out_specs=(hbm, vmem, hbm, hbm),
+        scratch_shapes=[
+            pltpu.VMEM(ret.shape, BF),
+            pltpu.VMEM((quarter_g, 2 * ff), BF),
+            pltpu.VMEM((quarter_g, 2 * ff), BF),
+            pltpu.VMEM((quarter_d, width), BF),
+            pltpu.VMEM((quarter_d, width), BF),
+            pltpu.VMEM((quarter_g, 2 * ff), F32),
+            pltpu.VMEM((quarter_d, width), F32),
+            pltpu.VMEM((tok_rows, width), F32),
+            dma((17,)),
+            dma((9,)),
+        ],
+        compiler_params=pltpu.CompilerParams(vmem_limit_bytes=VMEM_BYTES),
+    )(
+        ret, own_g, own_d, far_g, far_d,
+        routes.T, slot_index.T, route_weight.T, swap_flags[None],
+    )
+    return (grad_tokens, grad_weight.T, grad_gu[None], grad_dn[None])
 
 
 def solution(mesh):

time: 216 us -> 213 us (0.986); the launches traced: 213 us -> 213 us
  Pallas kernels: 206 us -> 212 us
  other arithmetic: 3.48 us -> 0 us
  local copies, waits for them, and re-layouts: 2.75 us -> 0 us
    pallas_call x1, Pallas kernels: 1.63 us -> 6.13 us  [body(): pl.pallas_call(finish_kernel, name='finish', out_shape=(jax.ShapeDtypeStr...]
    broadcast_in_dim x2 -> x0, other arithmetic: 3.48 us -> none  [the longest x1 2.11 us: body(): grad_gu = (own_g.astype(F32) + far_g.astype(F32))[None]]
    unnamed x18 -> x0, local copies, waits for them, and re-layouts: 2.75 us -> none
where the time goes in v3:
time: 213 us
  Pallas kernels  212 us (100%)
    pallas_call x1, Pallas kernels, body(): pl.pallas_call(functools.partial(exchange_kernel, parts, (experts, width,...  206 us
    pallas_call x1, Pallas kernels, body(): pl.pallas_call(finish_kernel, name='finish', out_shape=(jax.ShapeDtypeStr...  6.13 us

profile of v3, /device:TPU:1, one launch (start us, length us, event | category | flops | bytes accessed | tf_op | source)
XLA Modules:
  0.0 212.7 jit_solution(14434176647129888300)
XLA Ops:
  0.6 205.7 %ex_DWCGRS.1 = (bf16[64,16,1152]{2,1,0:T(8,128)(2,1)}, bf16[512,1536]{1,0:T(8,128)(2,1)}, bf16[192,2048]{1,0:T(8,128)(2,1)}, bf16[512,1536]{1,0:T(8,128)(2,1)}, bf16[192,2048]{1,0:T(8,128)(2,1)}) custom-call(s32[3,128]{1,0:T(4,128)} %bitcast.9, s32[3,128]{1,0:T(4,128)} %bitcast.11, f32[3,128]{1,0:T(4,128)} %bitcast.13, s32[1,64]{1,0:T(1,128)} %bitcast.15, ...), custom_call_target="tpu_custom_call" | custom-call | flops 14495514624 | bytes 12582912 | tf_op jit(solution)/shard_map/ex_DWCGRS/pallas_call | solution.py:563
  206.4 6.1 %finish.1 = (f32[128,2048]{1,0:T(8,128)}, f32[3,128]{1,0:T(4,128)}, f32[512,1536]{1,0:T(8,128)}, f32[192,2048]{1,0:T(8,128)}) custom-call(bf16[64,16,1152]{2,1,0:T(8,128)(2,1)} %get-tuple-element.13.ret_hbm, bf16[512,1536]{1,0:T(8,128)(2,1)} %get-tuple-element.14.own_g, bf16[192,2048]{1,0:T(8,128)(2,1)} %get-tuple-element.15.own_d, ...), custom_call_target="tpu_custom_call" | custom-call | tf_op jit(solution)/shard_map/finish/pallas_call | solution.py:609

commit v4 on v3

--- a/solution.py
+++ b/solution.py
@@ -385,20 +385,15 @@
     wide = pick_tile(2 * ff, 768)
     d_tile = pick_tile(quarter_g, 256)
 
-    def gate_up_grads(quarter):
+    def gate_up_grads(quarter, i):
         if "G" not in parts:
             return
-
-        def tile(i, carry):
-            start = pl.multiple_of(quarter * quarter_g + i * d_tile, d_tile)
-            left = rows_b[:, pl.ds(start, d_tile)]
-            for c in range(0, 2 * ff, wide):
-                part_g[pl.ds(start, d_tile), c : c + wide] = lax.dot_general(
-                    left, both_b[:, c : c + wide], COLS_BY_COLS, preferred_element_type=F32
-                ).astype(BF)
-            return carry
-
-        lax.fori_loop(0, quarter_g // d_tile, tile, 0)
+        start = pl.multiple_of(quarter * quarter_g + i * d_tile, d_tile)
+        left = rows_b[:, pl.ds(start, d_tile)]
+        for c in range(0, 2 * ff, wide):
+            part_g[pl.ds(start, d_tile), c : c + wide] = lax.dot_general(
+                left, both_b[:, c : c + wide], COLS_BY_COLS, preferred_element_type=F32
+            ).astype(BF)
 
     part_d = gathered
 
@@ -419,11 +414,10 @@
 
     reds = []
 
-    def to_sibling(slot, part, rows, landing, quarter, where):
-        if "S" not in parts:
-            return
+    def to_sibling(slot, part, rows, landing, quarter, where, off, count):
         copy = remote(
-            part.at[place_of(quarter, rows)], landing.at[where],
+            part.at[pl.ds(pl.multiple_of(quarter * rows + off, 16), count)],
+            landing.at[where, pl.ds(off, count)],
             red_send.at[slot], red_recv.at[slot], (sib, me),
         )
         copy.start()
@@ -431,36 +425,44 @@
 
     outs = []
 
-    def to_far(slot, part, rows, landing, out):
-        if "S" not in parts:
-            return
+    def to_far(slot, part, rows, landing, out, off, count):
         reds[slot].wait_recv()
-        total = part[place_of(far, rows), :].astype(F32) + landing[0].astype(F32)
-        landing[0] = total.astype(BF)
-        copy = remote(landing.at[0], out, out_send.at[slot], out_recv.at[slot], (far, me))
+        mine = part[pl.ds(pl.multiple_of(far * rows + off, 16), count), :].astype(F32)
+        place = pl.ds(off, count)
+        landing[0, place, :] = (mine + landing[0, place, :].astype(F32)).astype(BF)
+        copy = remote(
+            landing.at[0, place], out.at[place], out_send.at[slot], out_recv.at[slot], (far, me)
+        )
         copy.start()
         outs.append(copy)
 
-    gate_up_grads(far ^ 1)
-    to_sibling(0, part_g, quarter_g, sib_g, far ^ 1, 0)
-    gate_up_grads(far)
-    to_far(0, part_g, quarter_g, sib_g, far_g)
+    tiles = quarter_g // d_tile
+    for i in range(tiles):
+        gate_up_grads(far ^ 1, i)
+        to_sibling(i, part_g, quarter_g, sib_g, far ^ 1, 0, i * d_tile, d_tile)
+    for i in range(tiles):
+        gate_up_grads(far, i)
+        if i > 0:
+            to_far(i - 1, part_g, quarter_g, sib_g, far_g, (i - 1) * d_tile, d_tile)
+    to_far(tiles - 1, part_g, quarter_g, sib_g, far_g, (tiles - 1) * d_tile, d_tile)
     if "C" in parts:
         row_grads(ahead, block)
     give_back(last)
     down_grads()
-    to_sibling(1, part_d, quarter_d, sib_d, far ^ 1, 0)
-    to_sibling(2, part_d, quarter_d, sib_d, dp ^ 1, 1)
-    gate_up_grads(dp ^ 1)
-    to_sibling(3, part_g, quarter_g, sib_g, dp ^ 1, 1)
-    to_far(1, part_d, quarter_d, sib_d, far_d)
-    gate_up_grads(dp)
+    to_sibling(tiles, part_d, quarter_d, sib_d, far ^ 1, 0, 0, quarter_d)
+    to_sibling(tiles + 1, part_d, quarter_d, sib_d, dp ^ 1, 1, 0, quarter_d)
+    for i in range(tiles):
+        gate_up_grads(dp ^ 1, i)
+    to_sibling(tiles + 2, part_g, quarter_g, sib_g, dp ^ 1, 1, 0, quarter_g)
+    to_far(tiles, part_d, quarter_d, sib_d, far_d, 0, quarter_d)
+    for i in range(tiles):
+        gate_up_grads(dp, i)
     if "S" in parts:
-        reds[2].wait_recv()
+        reds[tiles + 1].wait_recv()
         own_d[...] = (
             part_d[place_of(dp, quarter_d), :].astype(F32) + sib_d[1].astype(F32)
         ).astype(BF)
-        reds[3].wait_recv()
+        reds[tiles + 2].wait_recv()
         own_g[...] = (
             part_g[place_of(dp, quarter_g), :].astype(F32) + sib_g[1].astype(F32)
         ).astype(BF)
@@ -594,7 +596,7 @@
             dma, dma((CHUNKS,)), dma, dma,
             dma((pieces,)), dma((pieces,)), dma((pieces,)), dma((pieces,)),
             dma((pieces,)), dma((pieces,)), dma((pieces,)), dma((pieces,)),
-            dma((4,)), dma((4,)), dma((2,)), dma((2,)),
+            dma((8,)), dma((8,)), dma((4,)), dma((4,)),
         ],
         compiler_params=pltpu.CompilerParams(
             has_side_effects=True, vmem_limit_bytes=VMEM_BYTES

time: 213 us -> 212 us (level)
  no operation moved by 1% of the time
where the time goes in v4:
time: 212 us
  Pallas kernels  211 us (100%)
    pallas_call x1, Pallas kernels, body(): pl.pallas_call(functools.partial(exchange_kernel, parts, (experts, width,...  205 us
    pallas_call x1, Pallas kernels, body(): pl.pallas_call(finish_kernel, name='finish', out_shape=(jax.ShapeDtypeStr...  6.13 us

profile of v4, /device:TPU:1, one launch (start us, length us, event | category | flops | bytes accessed | tf_op | source)
XLA Modules:
  0.0 212.2 jit_solution(15644644074880651855)
XLA Ops:
  0.6 205.2 %ex_DWCGRS.1 = (bf16[64,16,1152]{2,1,0:T(8,128)(2,1)}, bf16[512,1536]{1,0:T(8,128)(2,1)}, bf16[192,2048]{1,0:T(8,128)(2,1)}, bf16[512,1536]{1,0:T(8,128)(2,1)}, bf16[192,2048]{1,0:T(8,128)(2,1)}) custom-call(s32[3,128]{1,0:T(4,128)} %bitcast.9, s32[3,128]{1,0:T(4,128)} %bitcast.11, f32[3,128]{1,0:T(4,128)} %bitcast.13, s32[1,64]{1,0:T(1,128)} %bitcast.15, ...), custom_call_target="tpu_custom_call" | custom-call | flops 14495514624 | bytes 12582912 | tf_op jit(solution)/shard_map/ex_DWCGRS/pallas_call | solution.py:565
  205.9 6.1 %finish.1 = (f32[128,2048]{1,0:T(8,128)}, f32[3,128]{1,0:T(4,128)}, f32[512,1536]{1,0:T(8,128)}, f32[192,2048]{1,0:T(8,128)}) custom-call(bf16[64,16,1152]{2,1,0:T(8,128)(2,1)} %get-tuple-element.13.ret_hbm, bf16[512,1536]{1,0:T(8,128)(2,1)} %get-tuple-element.14.own_g, bf16[192,2048]{1,0:T(8,128)(2,1)} %get-tuple-element.15.own_d, ...), custom_call_target="tpu_custom_call" | custom-call | tf_op jit(solution)/shard_map/finish/pallas_call | solution.py:611

commit v5 on v4

--- a/solution.py
+++ b/solution.py
@@ -381,6 +381,8 @@
     if "C" in parts:
         forward_part(ahead, block)
         backward_part(ahead, block)
+        row_grads(ahead, block)
+    give_back(last)
 
     wide = pick_tile(2 * ff, 768)
     d_tile = pick_tile(quarter_g, 256)
@@ -445,9 +447,6 @@
         if i > 0:
             to_far(i - 1, part_g, quarter_g, sib_g, far_g, (i - 1) * d_tile, d_tile)
     to_far(tiles - 1, part_g, quarter_g, sib_g, far_g, (tiles - 1) * d_tile, d_tile)
-    if "C" in parts:
-        row_grads(ahead, block)
-    give_back(last)
     down_grads()
     to_sibling(tiles, part_d, quarter_d, sib_d, far ^ 1, 0, 0, quarter_d)
     to_sibling(tiles + 1, part_d, quarter_d, sib_d, dp ^ 1, 1, 0, quarter_d)

time: 212 us -> 215 us (1.014)
  Pallas kernels: 211 us -> 214 us
    pallas_call x1, Pallas kernels: 205 us -> 208 us  [body(): pl.pallas_call(functools.partial(exchange_kernel, parts, (experts, width,...]
where the time goes in v5:
time: 215 us
  Pallas kernels  214 us (100%)
    pallas_call x1, Pallas kernels, body(): pl.pallas_call(functools.partial(exchange_kernel, parts, (experts, width,...  208 us
    pallas_call x1, Pallas kernels, body(): pl.pallas_call(finish_kernel, name='finish', out_shape=(jax.ShapeDtypeStr...  6.14 us

profile of v5, /device:TPU:1, one launch (start us, length us, event | category | flops | bytes accessed | tf_op | source)
XLA Modules:
  0.0 214.5 jit_solution(15647607300333790182)
XLA Ops:
  0.6 207.6 %ex_DWCGRS.1 = (bf16[64,16,1152]{2,1,0:T(8,128)(2,1)}, bf16[512,1536]{1,0:T(8,128)(2,1)}, bf16[192,2048]{1,0:T(8,128)(2,1)}, bf16[512,1536]{1,0:T(8,128)(2,1)}, bf16[192,2048]{1,0:T(8,128)(2,1)}) custom-call(s32[3,128]{1,0:T(4,128)} %bitcast.9, s32[3,128]{1,0:T(4,128)} %bitcast.11, f32[3,128]{1,0:T(4,128)} %bitcast.13, s32[1,64]{1,0:T(1,128)} %bitcast.15, ...), custom_call_target="tpu_custom_call" | custom-call | flops 14495514624 | bytes 12582912 | tf_op jit(solution)/shard_map/ex_DWCGRS/pallas_call | solution.py:564
  208.2 6.1 %finish.1 = (f32[128,2048]{1,0:T(8,128)}, f32[3,128]{1,0:T(4,128)}, f32[512,1536]{1,0:T(8,128)}, f32[192,2048]{1,0:T(8,128)}) custom-call(bf16[64,16,1152]{2,1,0:T(8,128)(2,1)} %get-tuple-element.13.ret_hbm, bf16[512,1536]{1,0:T(8,128)(2,1)} %get-tuple-element.14.own_g, bf16[192,2048]{1,0:T(8,128)(2,1)} %get-tuple-element.15.own_d, ...), custom_call_target="tpu_custom_call" | custom-call | tf_op jit(solution)/shard_map/finish/pallas_call | solution.py:610
